TPU v7x, 32 devices: a whole 2x2x4 slice. The times are simulated.
32 devices in a mesh: blk: 16 (over z, y, x), aux: 2 (over core).
Axes of the slice: x: 2, y: 2, z: 4, core: 2. Of those that a mesh axis runs over, the one named last changes fastest.
Arguments:
- three_centre: bfloat16 [2048, 4, 4096], P('blk', 'aux'), may hold values from -6 to 6
- occupied_blocks: bfloat16 [128, 64, 64], P('blk'), may hold values from -1.5 to 1.5
- virtual_blocks: bfloat16 [128, 64, 64], P('blk'), may hold values from -1.5 to 1.5
- row_slot: int32 [2048], P('blk'), may hold values from 0 to 7
- col_slot: int32 [2048], P('blk'), may hold values from 0 to 7
- block_owner: int32 [2048, 1], P('blk'), may hold values from 0 to 15; in each aligned block of 128 rows (0 to 127, 128 to 255, ...) at most 16 rows name the same one
Outputs:
- polarizability: float32 [128, 4, 4], P('blk', 'aux')
Inputs may be any that keep to these rules, and one draw needn't show every extreme that they name: `block_owner`: among the 128 blocks stored on one index of blk, no owner is named more than 16 times, a bound that some block reaches.
All inputs are finite; a program needn't handle non-finite values.
Results may differ from a plain program's by a relative error of at most 0.0003.
Values may be sent and summed in bfloat16 or wider, within the bound.
No kernel may reach another device: no remote copies, remote signals or barrier semaphores. Data moves between devices by JAX's collectives and lax.ppermute only.
A program may use at most 64 MiB of HBM per device.

v0:
```python
import functools

import jax
import jax.numpy as jnp
from jax import lax
from jax.experimental import pallas as pl
from jax.experimental.pallas import tpu as pltpu
from jax.sharding import PartitionSpec as P

F32 = jnp.float32
BF16 = jnp.bfloat16
SMEM = pl.BlockSpec(memory_space=pltpu.SMEM)
VMEM = pl.BlockSpec(memory_space=pltpu.VMEM)
HBM = pl.BlockSpec(memory_space=pltpu.HBM)


def rounds_of(count):
    bits = count.bit_length() - 1
    found = []
    while bits:
        low = max(bits - 2, 0)
        found.append([step << low for step in range(1, 1 << (bits - low))])
        bits = low
    return found


def flip(values, distance, count):
    return lax.ppermute(values, "blk", [(i, i ^ distance) for i in range(count)])


def swap_cores(values):
    return lax.ppermute(values, "aux", [(0, 1), (1, 0)])


def split_flip(values, core_zero, core_one, count):
    pairs = [(2 * i + core, 2 * (i ^ distance) + core) for i in range(count) for core, distance in enumerate((core_zero, core_one))]
    return lax.ppermute(values, ("blk", "aux"), pairs)


def expand(occ_ref, expand_ref):
    groups, size, _ = occ_ref.shape
    wide = 2 * size
    column = lax.broadcasted_iota(jnp.int32, (size, wide), 1)
    mu = lax.broadcasted_iota(jnp.int32, (size, wide), 0)
    order = jnp.where(mu == (column % size) // 2 * 2 + column // size, 1.0, 0.0).astype(BF16)
    left = lax.broadcasted_iota(jnp.int32, (wide, wide), 0) // size
    same = left == lax.broadcasted_iota(jnp.int32, (wide, wide), 1) % 2
    for group in range(groups):
        occ = occ_ref[group]
        twice = jnp.concatenate([occ, occ], axis=1)
        spread = lax.dot_general(twice, order, (((0,), (0,)), ((), ())), preferred_element_type=F32)
        expand_ref[group] = jnp.where(same, spread, 0.0).astype(BF16)


def list_blocks(count, groups_dev, slots, owners, list_ref, column_ref):
    total = owners.shape[0]
    quarter = count // 4
    core = lax.axis_index("aux")
    me = lax.axis_index("blk")

    def clear(index, _):
        list_ref[index] = 0
        column_ref[index] = -1
        return 0

    lax.fori_loop(0, total, clear, 0, unroll=8)

    def add(block, found):
        away = owners[block] ^ me
        far = away // quarter
        place = (1 - (far & 1)) * quarter + (away & (quarter - 1))
        list_ref[found] = block
        column_ref[found] = place * groups_dev + slots[block]
        return found + jnp.where(((far ^ (far // 2)) & 1) == core, 1, 0)

    found = lax.fori_loop(0, total, add, jnp.int32(0), unroll=8)

    @pl.when(found < total)
    def _():
        list_ref[found] = 0
        column_ref[found] = -1

    list_ref[total] = found


def half_kernel(
    count, chunks, rows_ref, slots_ref, owners_ref, own_ref, other_ref, occ_ref,
    own_out, other_out, column_ref, list_ref,
    rows, slots, owners, own, occ, expand_ref, sems,
):
    groups_dev, wide, _ = expand_ref.shape
    size = wide // 2
    total = rows.shape[0]
    copies = [
        pltpu.make_async_copy(source, target, sems.at[index])
        for index, (source, target) in enumerate(
            [(owners_ref, owners), (slots_ref, slots), (rows_ref, rows), (occ_ref, occ), (own_ref, own)]
        )
    ]
    for copy in copies:
        copy.start()
    copies[0].wait()
    copies[1].wait()
    list_blocks(count, groups_dev, slots, owners, list_ref, column_ref)
    copies[3].wait()
    expand(occ, expand_ref)
    copies[2].wait()
    copies[4].wait()
    near = lax.broadcasted_iota(jnp.int32, (size, wide), 1) < size
    near_out = lax.broadcasted_iota(jnp.int32, (wide, wide), 1) < size

    def one(index):
        first, second = list_ref[2 * index], list_ref[2 * index + 1]
        first_row, second_row = rows[first], rows[second]
        stacked = []
        for source in (own, other_ref):
            one_block, two_block = source[first], source[second]
            one_turned = jnp.concatenate([one_block[:, size:], one_block[:, :size]], axis=1)
            two_turned = jnp.concatenate([two_block[:, size:], two_block[:, :size]], axis=1)
            stacked.append(jnp.concatenate(
                [jnp.where(near, one_block, two_turned), jnp.where(near, one_turned, two_block)], axis=0
            ))
        stacked = jnp.concatenate(stacked, axis=1)
        one_made = jnp.dot(expand_ref[first_row], stacked, preferred_element_type=F32)
        two_made = jnp.dot(expand_ref[second_row], stacked, preferred_element_type=F32)
        for part, out_ref in enumerate((own_out, other_out)):
            lanes = slice(part * wide, (part + 1) * wide)
            out_ref[index] = jnp.where(near_out, one_made[:, lanes], two_made[:, lanes]).astype(BF16)

    def work(indices, _):
        for index in indices:
            one(index)

    in_chunks(chunks, list_ref[total], work)


def in_chunks(chunks, count, work):
    start = 0
    for length in chunks:
        indices = range(start, start + length)
        if start:
            pl.when(count > 2 * start)(functools.partial(work, indices, False))
        else:
            work(indices, True)
        start += length


def chi_kernel(scale, chunks, list_ref, column_ref, own_ref, other_ref, virt_ref, out_ref, total_ref):
    _, wide, _ = own_ref.shape
    size = wide // 2
    places, tiles = virt_ref.shape[:2]
    groups_dev = 2 * tiles
    groups = places * groups_dev
    low = lax.broadcasted_iota(jnp.int32, (size, wide), 1) < size
    low_row = lax.broadcasted_iota(jnp.int32, (16, wide), 1) < size
    group_range = lax.broadcasted_iota(jnp.int32, (16, groups), 1)

    def virt_of(column, part):
        group = jnp.maximum(column, 0)
        found = virt_ref[group // groups_dev, group % groups_dev // 2]
        turned = jnp.concatenate([found[:, size:], found[:, :size]], axis=1)
        placed = jnp.where(group % 2 == part, found, turned)
        return jnp.where(low if part == 0 else ~low, placed, jnp.zeros_like(placed))

    def one(index, total):
        columns = [column_ref[2 * index], column_ref[2 * index + 1]]
        virt = jnp.concatenate([virt_of(column, part) for part, column in enumerate(columns)], axis=0)
        full = []
        for ref in (own_ref, other_ref):
            made = jnp.dot(ref[index], virt, preferred_element_type=F32).astype(BF16).astype(F32)
            full += [made[:size], made[size:]]
        sums = {}
        for p in range(4):
            for q in range(p, 4):
                sums[p, q] = sums[q, p] = jnp.sum(full[p] * full[q], axis=0, keepdims=True)
        rows = [sums[p, q] for p in range(2) for q in range(4)]
        rows += [sums[p, q ^ 2] for p in range(2, 4) for q in range(4)]
        values = jnp.concatenate(rows, axis=0)
        for column, where in zip(columns, (low_row, ~low_row)):
            value = jnp.sum(jnp.where(where, values, 0.0), axis=1, keepdims=True)
            total = total + jnp.where(group_range == column, value, 0.0)
        return total

    def work(indices, is_first):
        total = jnp.zeros((16, groups), F32)
        for index in indices:
            total = one(index, total)
        total_ref[...] = total if is_first else total_ref[...] + total

    in_chunks(chunks, list_ref[list_ref.shape[0] - 1], work)
    summed = total_ref[...] * scale
    rows = 8 * groups_dev
    lane = lax.broadcasted_iota(jnp.int32, (8, 2 * rows), 1) // groups_dev % 8
    sublane = lax.broadcasted_iota(jnp.int32, (8, 2 * rows), 0)
    quarter = places // 2
    core = lax.axis_index("aux")
    me = lax.axis_index("blk")
    out_ref[...] = jnp.zeros(out_ref.shape, F32)
    for target in range(2):
        wanted = jnp.where(core == target, summed[:8], summed[8:])
        if target:
            wanted = jnp.concatenate([wanted[2:4], wanted[:2], wanted[6:], wanted[4:6]], axis=0)
        for start in range(0, places, 8):
            piece = wanted[:, start * groups_dev:(start + 8) * groups_dev]
            piece = jnp.concatenate([piece, piece], axis=1)
            turned = jnp.zeros_like(piece)
            for shift in range(8):
                moved = pltpu.roll(pltpu.roll(piece, shift, 0), (2 * rows - groups_dev * shift) % (2 * rows), 1)
                turned = jnp.where(lane == (sublane + 8 - shift) % 8, moved, turned)
            for index in range(8):
                place = start + index
                second = place // quarter
                far = jnp.where(core == 0, 3 - 3 * second, 1 + second)
                owner = me ^ (far * quarter + place % quarter)
                out_ref[pl.ds(2 * owner + target, 1), :] = turned[index:index + 1, :rows]


def body(count, three_centre, occupied_blocks, virtual_blocks, row_slot, col_slot, block_owner):
    block_count, aux_local, width = three_centre.shape
    groups_dev, size, _ = occupied_blocks.shape
    scale = 0.25 / (size * size)
    wide = 2 * size
    pairs = block_count // 4
    core = lax.axis_index("aux")
    rounds = rounds_of(count)
    near, mid, far = rounds[0]

    def by_mu(values):
        found = values.reshape(block_count, aux_local, width // wide, wide)
        return found.transpose(0, 2, 1, 3).reshape(block_count, size, wide)

    def in_hbm(values):
        return pltpu.with_memory_space_constraint(values, pltpu.HBM)

    chunks = (pairs,) + (8,) * (pairs // 8)
    virt = jnp.concatenate([virtual_blocks[0::2], virtual_blocks[1::2]], axis=2)
    other = swap_cores(by_mu(three_centre))
    virt = jnp.stack([split_flip(virt, far, near, count), split_flip(virt, 0, mid, count)])
    virt, rows = lax.optimization_barrier((virt, row_slot))
    half_shape = jax.ShapeDtypeStruct((2 * pairs, wide, wide), BF16)
    integers = pltpu.SMEM((block_count,), jnp.int32)
    own_half, other_half, columns, block_list = pl.pallas_call(
        functools.partial(half_kernel, count, chunks),
        out_shape=[
            half_shape,
            half_shape,
            jax.ShapeDtypeStruct((block_count,), jnp.int32),
            jax.ShapeDtypeStruct((block_count + 1,), jnp.int32),
        ],
        in_specs=[HBM] * 4 + [VMEM, HBM],
        out_specs=[VMEM, VMEM, SMEM, SMEM],
        scratch_shapes=[
            integers,
            integers,
            integers,
            pltpu.VMEM((block_count, size, wide), BF16),
            pltpu.VMEM((groups_dev, size, size), BF16),
            pltpu.VMEM((groups_dev, wide, wide), BF16),
            pltpu.SemaphoreType.DMA((5,)),
        ],
        compiler_params=pltpu.CompilerParams(vmem_limit_bytes=16 * 1024 * 1024),
        cost_estimate=pl.CostEstimate(flops=10**9, bytes_accessed=4 * 1024 * 1024, transcendentals=0),
        name="half",
    )(
        in_hbm(rows), in_hbm(col_slot), in_hbm(block_owner.reshape(block_count)),
        in_hbm(by_mu(three_centre)), other, in_hbm(occupied_blocks),
    )
    for distances in rounds[1:]:
        arrived = [flip(virt, distance, count) for distance in distances]
        if distances is rounds[-1]:
            arrived, own_half = lax.optimization_barrier((arrived, own_half))
        virt = jnp.stack([virt] + arrived, axis=1).reshape((-1,) + virt.shape[1:])

    places = count // 2
    partial = pl.pallas_call(
        functools.partial(chi_kernel, scale, chunks),
        out_shape=jax.ShapeDtypeStruct((2 * count, 8 * groups_dev), F32),
        in_specs=[SMEM, SMEM] + [VMEM] * 3,
        out_specs=VMEM,
        scratch_shapes=[pltpu.VMEM((16, places * groups_dev), F32)],
        compiler_params=pltpu.CompilerParams(vmem_limit_bytes=16 * 1024 * 1024),
        cost_estimate=pl.CostEstimate(flops=10**9, bytes_accessed=4 * 1024 * 1024, transcendentals=0),
        name="chi",
    )(block_list, columns, own_half, other_half, virt)

    arrived = lax.all_to_all(partial, ("blk", "aux"), 0, 0, tiled=True)
    return jnp.sum(arrived, axis=0).reshape(2, 4, groups_dev).transpose(2, 0, 1)


def solution(mesh):
    in_specs = (
        P("blk", "aux", None),
        P("blk", None, None),
        P("blk", None, None),
        P("blk"),
        P("blk"),
        P("blk", None),
    )
    out_specs = P("blk", "aux", None)
    return jax.shard_map(
        functools.partial(body, mesh.shape["blk"]),
        mesh=mesh,
        in_specs=in_specs,
        out_specs=out_specs,
        check_vma=False,
    )
```

profile of v0, /device:TPU:0, one launch (start us, length us, event | category | flops | bytes accessed | tf_op | source)
XLA Modules:
  0.0 34.3 jit_solution(1200603214892304833)
XLA Ops:
  0.0 0.5 %collective-permute-start.2 = (bf16[128,64,128]{2,1,0:T(8,128)(2,1)}, bf16[128,64,128]{2,1,0:T(8,128)(2,1)S(1)}, u32[]{:S(2)}, u32[]{:S(2)}) collective-permute-start(bf16[128,64,128]{2,1,0:T(8,128)(2,1)} %bitcast.19), channel_id=1, source_target_pairs={{0,1},{1,0},{2,3},{3,2},{4,5},{5,4},{6,7},{7,6},{8,9},{9,8},{10,11... | collective-permute-start | bytes 6291464 | tf_op jit(solution)/shard_map/ppermute | solution.py:32
  0.5 0.9 %fusion = (bf16[4,64,64]{2,1,0:T(8,128)(2,1)S(1)}, bf16[4,64,64]{2,1,0:T(8,128)(2,1)S(1)}) fusion(bf16[8,64,64]{2,1,0:T(8,128)(2,1)} %param.8), kind=kLoop, calls=%fused_computation.3 | loop fusion | bytes 131072 | tf_op jit(solution)/shard_map/slice | solution.py:236
  1.3 0.1 pad_maximum_fusion.2
  1.4 4.7 %collective-permute-start = (bf16[4,64,128]{2,1,0:T(8,128)(2,1)S(1)}, bf16[4,64,128]{2,1,0:T(8,128)(2,1)S(1)}, u32[]{:S(2)}, u32[]{:S(2)}) collective-permute-start(bf16[4,64,128]{2,1,0:T(8,128)(2,1)S(1)} %pad_maximum_fusion.2), channel_id=1, source_target_pairs={{0,24},{1,9},{2,26},{3,11},{4,28},{5,13},{6,30},{7,15},{8,16},{9,1... | collective-permute-start | bytes 196616 | tf_op jit(solution)/shard_map/ppermute | solution.py:37
  6.1 0.7 %collective-permute-start.1 = (bf16[4,64,128]{2,1,0:T(8,128)(2,1)S(1)}, bf16[4,64,128]{2,1,0:T(8,128)(2,1)S(1)}, u32[]{:S(2)}, u32[]{:S(2)}) collective-permute-start(bf16[4,64,128]{2,1,0:T(8,128)(2,1)S(1)} %pad_maximum_fusion.2), channel_id=1, source_target_pairs={{0,0},{1,17},{2,2},{3,19},{4,4},{5,21},{6,6},{7,23},{8,8},{9,25},{... | collective-permute-start | bytes 196616 | tf_op jit(solution)/shard_map/ppermute | solution.py:37
  6.8 2.3 %collective-permute-done = bf16[4,64,128]{2,1,0:T(8,128)(2,1)S(1)} collective-permute-done((bf16[4,64,128]{2,1,0:T(8,128)(2,1)S(1)}, bf16[4,64,128]{2,1,0:T(8,128)(2,1)S(1)}, u32[]{:S(2)}, u32[]{:S(2)}) %collective-permute-start) | collective-permute-done | bytes 65568 | tf_op jit(solution)/shard_map/ppermute | solution.py:37
  9.0 0.0 collective-permute-done.1
  9.1 1.6 %collective-permute-start.3 = (bf16[2,4,64,128]{3,2,1,0:T(8,128)(2,1)S(1)}, bf16[2,4,64,128]{3,2,1,0:T(8,128)(2,1)S(1)}, u32[]{:S(2)}, u32[]{:S(2)}) collective-permute-start(bf16[2,4,64,128]{3,2,1,0:T(8,128)(2,1)S(1)} %pad_maximum_fusion.1), channel_id=1, source_target_pairs={{0,2},{2,0},{4,6},{6,4},{8,10},{10,8},{12,14},{14,12},{16,18},{18,... | collective-permute-start | bytes 393224 | tf_op jit(solution)/shard_map/ppermute | solution.py:28
  10.6 1.5 %collective-permute-start.4 = (bf16[2,4,64,128]{3,2,1,0:T(8,128)(2,1)S(1)}, bf16[2,4,64,128]{3,2,1,0:T(8,128)(2,1)S(1)}, u32[]{:S(2)}, u32[]{:S(2)}) collective-permute-start(bf16[2,4,64,128]{3,2,1,0:T(8,128)(2,1)S(1)} %pad_maximum_fusion.1), channel_id=1, source_target_pairs={{0,4},{2,6},{4,0},{6,2},{8,12},{10,14},{12,8},{14,10},{16,20},{18,... | collective-permute-start | bytes 393224 | tf_op jit(solution)/shard_map/ppermute | solution.py:28
  12.1 0.5 %collective-permute-start.5 = (bf16[2,4,64,128]{3,2,1,0:T(8,128)(2,1)S(1)}, bf16[2,4,64,128]{3,2,1,0:T(8,128)(2,1)S(1)}, u32[]{:S(2)}, u32[]{:S(2)}) collective-permute-start(bf16[2,4,64,128]{3,2,1,0:T(8,128)(2,1)S(1)} %pad_maximum_fusion.1), channel_id=1, source_target_pairs={{0,6},{2,4},{4,2},{6,0},{8,14},{10,12},{12,10},{14,8},{16,22},{18,... | collective-permute-start | bytes 393224 | tf_op jit(solution)/shard_map/ppermute | solution.py:28
  12.6 0.0 collective-permute-done.2.other_ref
  12.6 5.1 %half.1 = (bf16[64,128,128]{2,1,0:T(8,128)(2,1)S(1)}, bf16[64,128,128]{2,1,0:T(8,128)(2,1)S(1)}, s32[128]{0:T(128)S(1)}, s32[129]{0:T(256)S(1)}) custom-call(s32[128]{0:T(128)} %rows_ref, s32[128]{0:T(128)} %slots_ref.1, s32[128]{0:T(128)} %bitcast.27, bf16[128,64,128]{2,1,0:T(8,128)(2,1)} %bitcast.20, ...), custom_call_target="tpu_custom_call" | custom-call | flops 1000000000 | bytes 4194304 | tf_op jit(solution)/shard_map/half/pallas_call | solution.py:242
  17.8 0.0 collective-permute-done.3
  17.8 0.6 %collective-permute-done.4 = bf16[2,4,64,128]{3,2,1,0:T(8,128)(2,1)S(1)} collective-permute-done((bf16[2,4,64,128]{3,2,1,0:T(8,128)(2,1)S(1)}, bf16[2,4,64,128]{3,2,1,0:T(8,128)(2,1)S(1)}, u32[]{:S(2)}, u32[]{:S(2)}) %collective-permute-start.4) | collective-permute-done | bytes 131104 | tf_op jit(solution)/shard_map/ppermute | solution.py:28
  18.4 0.9 %collective-permute-done.5 = bf16[2,4,64,128]{3,2,1,0:T(8,128)(2,1)S(1)} collective-permute-done((bf16[2,4,64,128]{3,2,1,0:T(8,128)(2,1)S(1)}, bf16[2,4,64,128]{3,2,1,0:T(8,128)(2,1)S(1)}, u32[]{:S(2)}, u32[]{:S(2)}) %collective-permute-start.5) | collective-permute-done | bytes 131104 | tf_op jit(solution)/shard_map/ppermute | solution.py:28
  19.3 0.1 pad_maximum_fusion
  19.4 2.9 %chi.1 = f32[32,64]{1,0:T(8,128)S(1)} custom-call(s32[129]{0:T(256)S(1)} %get-tuple-element.16.list_ref, s32[128]{0:T(128)S(1)} %get-tuple-element.17.column_ref, bf16[64,128,128]{2,1,0:T(8,128)(2,1)S(1)} %get-tuple-element.20.own_ref, bf16[64,128,128]{2,1,0:T(8,128)(2,1)S(1)} %get-tuple-element.21.other_ref, bf16[8,4,64,128]{3,2,1,0:T(8,128)(2,1)S(1)} %bitcast.17), custom_call_target="tpu_custom_call" | custom-call | flops 1000000000 | bytes 4194304 | tf_op jit(solution)/shard_map/chi/pallas_call | solution.py:275
  22.3 11.3 %all_to_all.9 = f32[32,1,64]{2,1,0:T(1,128)S(1)} all-to-all(f32[32,1,64]{2,1,0:T(1,128)S(1)} %bitcast.18), channel_id=1, replica_groups=mesh['blk'=16,'aux'=2] {'blk','aux'}, dimensions={0} | all-to-all | bytes 16384 | tf_op jit(solution)/shard_map/all_to_all | solution.py:286
  33.6 0.1 reduce_sum.9
  33.6 0.7 %reshape.23 = f32[2,4,8]{2,1,0:T(4,128)} reshape(f32[64]{0:T(128)S(1)} %reduce_sum.9) | data formatting | bytes 512 | tf_op jit(solution)/shard_map/reshape | solution.py:287
  (2 shorter events, 0.1 us)
Async XLA Ops:
  0.0 12.6 %collective-permute-start.2 = (bf16[128,64,128]{2,1,0:T(8,128)(2,1)}, bf16[128,64,128]{2,1,0:T(8,128)(2,1)S(1)}, u32[]{:S(2)}, u32[]{:S(2)}) collective-permute-start(bf16[128,64,128]{2,1,0:T(8,128)(2,1)} %bitcast.19), channel_id=1, source_target_pairs={{0,1},{1,0},{2,3},{3,2},{4,5},{5,4},{6,7},{7,6},{8,9},{9,8},{10,11... | collective-permute-start | bytes 6291464 | tf_op jit(solution)/shard_map/ppermute | solution.py:32
  1.4 7.6 %collective-permute-start = (bf16[4,64,128]{2,1,0:T(8,128)(2,1)S(1)}, bf16[4,64,128]{2,1,0:T(8,128)(2,1)S(1)}, u32[]{:S(2)}, u32[]{:S(2)}) collective-permute-start(bf16[4,64,128]{2,1,0:T(8,128)(2,1)S(1)} %pad_maximum_fusion.2), channel_id=1, source_target_pairs={{0,24},{1,9},{2,26},{3,11},{4,28},{5,13},{6,30},{7,15},{8,16},{9,1... | collective-permute-start | bytes 196616 | tf_op jit(solution)/shard_map/ppermute | solution.py:37
  6.1 2.9 %collective-permute-start.1 = (bf16[4,64,128]{2,1,0:T(8,128)(2,1)S(1)}, bf16[4,64,128]{2,1,0:T(8,128)(2,1)S(1)}, u32[]{:S(2)}, u32[]{:S(2)}) collective-permute-start(bf16[4,64,128]{2,1,0:T(8,128)(2,1)S(1)} %pad_maximum_fusion.2), channel_id=1, source_target_pairs={{0,0},{1,17},{2,2},{3,19},{4,4},{5,21},{6,6},{7,23},{8,8},{9,25},{... | collective-permute-start | bytes 196616 | tf_op jit(solution)/shard_map/ppermute | solution.py:37
  9.1 8.7 %collective-permute-start.3 = (bf16[2,4,64,128]{3,2,1,0:T(8,128)(2,1)S(1)}, bf16[2,4,64,128]{3,2,1,0:T(8,128)(2,1)S(1)}, u32[]{:S(2)}, u32[]{:S(2)}) collective-permute-start(bf16[2,4,64,128]{3,2,1,0:T(8,128)(2,1)S(1)} %pad_maximum_fusion.1), channel_id=1, source_target_pairs={{0,2},{2,0},{4,6},{6,4},{8,10},{10,8},{12,14},{14,12},{16,18},{18,... | collective-permute-start | bytes 393224 | tf_op jit(solution)/shard_map/ppermute | solution.py:28
  10.6 7.8 %collective-permute-start.4 = (bf16[2,4,64,128]{3,2,1,0:T(8,128)(2,1)S(1)}, bf16[2,4,64,128]{3,2,1,0:T(8,128)(2,1)S(1)}, u32[]{:S(2)}, u32[]{:S(2)}) collective-permute-start(bf16[2,4,64,128]{3,2,1,0:T(8,128)(2,1)S(1)} %pad_maximum_fusion.1), channel_id=1, source_target_pairs={{0,4},{2,6},{4,0},{6,2},{8,12},{10,14},{12,8},{14,10},{16,20},{18,... | collective-permute-start | bytes 393224 | tf_op jit(solution)/shard_map/ppermute | solution.py:28
  12.1 7.1 %collective-permute-start.5 = (bf16[2,4,64,128]{3,2,1,0:T(8,128)(2,1)S(1)}, bf16[2,4,64,128]{3,2,1,0:T(8,128)(2,1)S(1)}, u32[]{:S(2)}, u32[]{:S(2)}) collective-permute-start(bf16[2,4,64,128]{3,2,1,0:T(8,128)(2,1)S(1)} %pad_maximum_fusion.1), channel_id=1, source_target_pairs={{0,6},{2,4},{4,2},{6,0},{8,14},{10,12},{12,10},{14,8},{16,22},{18,... | collective-permute-start | bytes 393224 | tf_op jit(solution)/shard_map/ppermute | solution.py:28
where the time goes:
time: 34.5 us; the launch traced here: 34.3 us
  blocking collectives  11.3 us (33%)
  starting transfers between devices  9.32 us (27%)
  Pallas kernels  8.02 us (23%)
  waiting for transfers between devices  3.77 us (11%)
  local copies, waits for them, and re-layouts  1.61 us (5%)
    all_to_all x1, blocking collectives, body(): arrived = lax.all_to_all(partial, ('blk', 'aux'), 0, 0, tiled=True)  11.3 us
    ppermute x2, starting transfers between devices, split_flip(): return lax.ppermute(values, ('blk', 'aux'), pairs)  5.32 us
    pallas_call x1, Pallas kernels, body(): pl.pallas_call(functools.partial(half_kernel, count, chunks), out_shape=[...  5.15 us
    ppermute x3, starting transfers between devices, flip(): lax.ppermute(values, 'blk', [(i, i ^ distance) for i in range(count)])  3.55 us
    pallas_call x1, Pallas kernels, body(): pl.pallas_call(functools.partial(chi_kernel, scale, chunks), out_shape=ja...  2.88 us
    ppermute x2, waiting for transfers between devices, split_flip(): return lax.ppermute(values, ('blk', 'aux'), pairs)  2.27 us
    ppermute x3, waiting for transfers between devices, flip(): lax.ppermute(values, 'blk', [(i, i ^ distance) for i in range(count)])  1.5 us
    slice x1, local copies, waits for them, and re-layouts, body(): virt = jnp.concatenate([virtual_blocks[0::2], virtual_blocks[1::2]], axis=2)  0.88 us
  transfers between devices with their start and end apart: 6, of which 3 were waited for; matrix products, arithmetic and copies ran while one was open for 3% of the time, Pallas kernels for 15%

commit v1 on v0

v1 whole, which is shorter than its diff:
```python
import functools

import jax
import jax.numpy as jnp
from jax import lax
from jax.experimental import pallas as pl
from jax.experimental.pallas import tpu as pltpu
from jax.sharding import PartitionSpec as P

F32 = jnp.float32
BF16 = jnp.bfloat16
SMEM = pl.BlockSpec(memory_space=pltpu.SMEM)
VMEM = pl.BlockSpec(memory_space=pltpu.VMEM)
HBM = pl.BlockSpec(memory_space=pltpu.HBM)


def rounds_of(count):
    bits = count.bit_length() - 1
    found = []
    while bits:
        low = max(bits - 2, 0)
        found.append([step << low for step in range(1, 1 << (bits - low))])
        bits = low
    return found


def flip(values, distance, count):
    return lax.ppermute(values, "blk", [(i, i ^ distance) for i in range(count)])


def swap_cores(values):
    return lax.ppermute(values, "aux", [(0, 1), (1, 0)])


def split_flip(values, core_zero, core_one, count):
    pairs = [(2 * i + core, 2 * (i ^ distance) + core) for i in range(count) for core, distance in enumerate((core_zero, core_one))]
    return lax.ppermute(values, ("blk", "aux"), pairs)


def expand(occ_ref, expand_ref):
    groups, size, _ = occ_ref.shape
    wide = 2 * size
    column = lax.broadcasted_iota(jnp.int32, (size, wide), 1)
    mu = lax.broadcasted_iota(jnp.int32, (size, wide), 0)
    order = jnp.where(mu == (column % size) // 2 * 2 + column // size, 1.0, 0.0).astype(BF16)
    left = lax.broadcasted_iota(jnp.int32, (wide, wide), 0) // size
    same = left == lax.broadcasted_iota(jnp.int32, (wide, wide), 1) % 2
    for group in range(groups):
        occ = occ_ref[group]
        twice = jnp.concatenate([occ, occ], axis=1)
        spread = lax.dot_general(twice, order, (((0,), (0,)), ((), ())), preferred_element_type=F32)
        expand_ref[group] = jnp.where(same, spread, 0.0).astype(BF16)


def bits_of(size):
    return size.bit_length() - 1


def list_blocks(count, late_bit, owners, list_ref):
    total = owners.shape[0]
    quarter = count // 4
    core = lax.axis_index("aux")
    me = lax.axis_index("blk") ^ quarter

    def add(block, found):
        early, late = found
        away = owners[block] ^ me
        mine = (((away + quarter) >> (bits_of(quarter) + 1)) & 1) ^ core
        late_here = mine & (away >> late_bit)
        list_ref[jnp.where((away >> late_bit) & 1 == 1, late, early)] = block
        return early + mine - late_here, late + late_here

    early, late = lax.fori_loop(0, total, add, (jnp.int32(0), jnp.int32(total)), unroll=8)
    list_ref[2 * total] = early
    list_ref[2 * total + 1] = late - total


def ready_kernel(
    count, late_bit, rows_ref, slots_ref, owners_ref, occ_ref, expand_ref, list_ref, rows, slots, owners, occ, sems
):
    copies = [
        pltpu.make_async_copy(source, target, sems.at[index])
        for index, (source, target) in enumerate(
            [(owners_ref, owners), (slots_ref, slots), (rows_ref, rows), (occ_ref, occ)]
        )
    ]
    for copy in copies:
        copy.start()

    def clear(index, _):
        list_ref[index] = 0
        return 0

    lax.fori_loop(0, list_ref.shape[0], clear, 0, unroll=43)
    copies[0].wait()
    list_blocks(count, late_bit, owners, list_ref)
    copies[3].wait()
    expand(occ, expand_ref)
    copies[1].wait()
    copies[2].wait()


def half_kernel(chunks, list_ref, rows, own_ref, other_ref, expand_ref, *out_refs):
    total = own_ref.shape[0]
    wide = expand_ref.shape[1]
    size = wide // 2
    near = lax.broadcasted_iota(jnp.int32, (size, wide), 1) < size
    near_out = lax.broadcasted_iota(jnp.int32, (wide, wide), 1) < size

    def one(late, index):
        first, second = [list_ref[late * total + 2 * index + part] for part in range(2)]
        stacked = []
        for source in (own_ref, other_ref):
            one_block, two_block = source[first], source[second]
            one_turned = jnp.concatenate([one_block[:, size:], one_block[:, :size]], axis=1)
            two_turned = jnp.concatenate([two_block[:, size:], two_block[:, :size]], axis=1)
            stacked.append(jnp.concatenate(
                [jnp.where(near, one_block, two_turned), jnp.where(near, one_turned, two_block)], axis=0
            ))
        stacked = jnp.concatenate(stacked, axis=1)
        made = [jnp.dot(expand_ref[rows[block]], stacked, preferred_element_type=F32) for block in (first, second)]
        for part, out_ref in enumerate(out_refs[2 * late:2 * late + 2]):
            lanes = slice(part * wide, (part + 1) * wide)
            out_ref[index] = jnp.where(near_out, made[0][:, lanes], made[1][:, lanes]).astype(BF16)

    for late in range(2):
        def work(indices, _, late=late):
            for index in indices:
                one(late, index)

        in_chunks(chunks, list_ref[2 * total + late], work)


def in_chunks(chunks, count, work):
    start = 0
    for length in chunks:
        indices = range(start, start + length)
        if start:
            pl.when(count > 2 * start)(functools.partial(work, indices, False))
        else:
            work(indices, True)
        start += length


def add_chi(late, chunks, list_ref, slots, owners, own_ref, other_ref, virt_ref, total_ref):
    _, wide, _ = own_ref.shape
    size = wide // 2
    turns, places, tiles = virt_ref.shape[:3]
    groups_dev = 2 * tiles
    groups = total_ref.shape[1]
    all_turns = groups // (places * groups_dev)
    total_blocks = owners.shape[0]
    count = list_ref[2 * total_blocks + late]
    me = lax.axis_index("blk") ^ (places * all_turns // 2)
    low = lax.broadcasted_iota(jnp.int32, (size, wide), 1) < size
    low_row = lax.broadcasted_iota(jnp.int32, (16, wide), 1) < size
    group_range = lax.broadcasted_iota(jnp.int32, (16, groups), 1)

    core = lax.axis_index("aux")

    def virt_of(place, slot, part):
        found = virt_ref[place & (turns - 1), place >> bits_of(all_turns), slot & (tiles - 1)]
        turned = jnp.concatenate([found[:, size:], found[:, :size]], axis=1)
        placed = jnp.where((slot // tiles) ^ core == part, found, turned)
        return jnp.where(low if part == 0 else ~low, placed, jnp.zeros_like(placed))

    def one(index, total):
        blocks = [list_ref[late * total_blocks + 2 * index + part] for part in range(2)]
        found = [(owners[block] ^ me) & (places * all_turns - 1) for block in blocks]
        columns = [place * groups_dev + slots[block] for place, block in zip(found, blocks)]
        virt = jnp.concatenate([virt_of(place, slots[block], part) for part, (place, block) in enumerate(zip(found, blocks))], axis=0)
        full = []
        for ref in (own_ref, other_ref):
            made = jnp.dot(ref[index], virt, preferred_element_type=F32).astype(BF16).astype(F32)
            full += [made[:size], made[size:]]
        sums = {}
        for p in range(4):
            for q in range(p, 4):
                sums[p, q] = sums[q, p] = jnp.sum(full[p] * full[q], axis=0, keepdims=True)
        rows = [sums[p, q] for p in range(2) for q in range(4)]
        rows += [sums[p, q ^ 2] for p in range(2, 4) for q in range(4)]
        values = jnp.concatenate(rows, axis=0)
        for part, where in enumerate((low_row, ~low_row)):
            column = jnp.where(2 * index + part < count, columns[part], -1)
            value = jnp.sum(jnp.where(where, values, 0.0), axis=1, keepdims=True)
            total = total + jnp.where(group_range == column, value, 0.0)
        return total

    def work(indices, is_first):
        total = jnp.zeros((16, groups), F32)
        for index in indices:
            total = one(index, total)
        total_ref[...] = total if is_first and not late else total_ref[...] + total

    in_chunks(chunks, count, work)


def early_kernel(chunks, list_ref, slots, owners, own_ref, other_ref, virt_ref, total_ref):
    add_chi(0, chunks, list_ref, slots, owners, own_ref, other_ref, virt_ref, total_ref)


def late_kernel(scale, chunks, list_ref, slots, owners, own_ref, other_ref, virt_ref, early_ref, out_ref, total_ref):
    total_ref[...] = early_ref[...]
    add_chi(1, chunks, list_ref, slots, owners, own_ref, other_ref, virt_ref, total_ref)
    summed = total_ref[...] * scale
    groups_dev = 2 * virt_ref.shape[2]
    places = summed.shape[1] // groups_dev
    rows = 8 * groups_dev
    lane = lax.broadcasted_iota(jnp.int32, (8, 2 * rows), 1) // groups_dev % 8
    sublane = lax.broadcasted_iota(jnp.int32, (8, 2 * rows), 0)
    quarter = places // 2
    core = lax.axis_index("aux")
    me = lax.axis_index("blk")
    out_ref[...] = jnp.zeros(out_ref.shape, F32)
    for target in range(2):
        wanted = jnp.where(core == target, summed[:8], summed[8:])
        if target:
            wanted = jnp.concatenate([wanted[2:4], wanted[:2], wanted[6:], wanted[4:6]], axis=0)
        for start in range(0, places, 8):
            piece = wanted[:, start * groups_dev:(start + 8) * groups_dev]
            piece = jnp.concatenate([piece, piece], axis=1)
            turned = jnp.zeros_like(piece)
            for shift in range(8):
                moved = pltpu.roll(pltpu.roll(piece, shift, 0), (2 * rows - groups_dev * shift) % (2 * rows), 1)
                turned = jnp.where(lane == (sublane + 8 - shift) % 8, moved, turned)
            for index in range(8):
                place = start + index
                second = place // quarter
                far = jnp.where(core == 0, 3 - 3 * second, 1 + second)
                owner = me ^ (far * quarter + place % quarter)
                out_ref[pl.ds(2 * owner + target, 1), :] = turned[index:index + 1, :rows]


def body(count, three_centre, occupied_blocks, virtual_blocks, row_slot, col_slot, block_owner):
    block_count, aux_local, width = three_centre.shape
    groups_dev, size, _ = occupied_blocks.shape
    scale = 0.25 / (size * size)
    wide = 2 * size
    pairs = block_count // 4
    core = lax.axis_index("aux")
    rounds = rounds_of(count)
    near, mid, far = rounds[0]

    def by_mu(values):
        found = values.reshape(block_count, aux_local, width // wide, wide)
        return found.transpose(0, 2, 1, 3).reshape(block_count, size, wide)

    def in_hbm(values):
        return pltpu.with_memory_space_constraint(values, pltpu.HBM)

    chunks = (5 * pairs // 8,) + (pairs // 8,) * 3 + (pairs // 4,) * 4
    tiles = groups_dev // 2
    left = lax.dynamic_slice_in_dim(virtual_blocks, core * tiles, tiles)
    left, whole = lax.optimization_barrier((left, virtual_blocks))
    virt = jnp.concatenate([left, lax.dynamic_slice_in_dim(whole, (1 - core) * tiles, tiles)], axis=2)
    other = swap_cores(by_mu(three_centre))
    arrived = [split_flip(virt, far, near, count), split_flip(virt, 0, mid, count)]
    integers = pltpu.SMEM((block_count,), jnp.int32)
    options = dict(
        compiler_params=pltpu.CompilerParams(vmem_limit_bytes=16 * 1024 * 1024),
        cost_estimate=pl.CostEstimate(flops=10**9, bytes_accessed=4 * 1024 * 1024, transcendentals=0),
    )
    all_turns = len(rounds[-1]) + 1
    expanded, block_list, rows, slots, owners = pl.pallas_call(
        functools.partial(ready_kernel, count, bits_of(all_turns) - 1),
        out_shape=[
            jax.ShapeDtypeStruct((groups_dev, wide, wide), BF16),
            pltpu.SMEM((2 * block_count + 2,), jnp.int32),
            integers,
            integers,
            integers,
        ],
        in_specs=[HBM] * 4,
        out_specs=[VMEM] + [SMEM] * 4,
        scratch_shapes=[pltpu.VMEM((groups_dev, size, size), BF16), pltpu.SemaphoreType.DMA((4,))],
        name="ready",
        **options,
    )(in_hbm(row_slot), in_hbm(col_slot), in_hbm(block_owner.reshape(block_count)), in_hbm(occupied_blocks))
    arrived, expanded = lax.optimization_barrier((arrived, expanded))
    virt = jnp.stack(arrived)
    half_shape = jax.ShapeDtypeStruct((2 * pairs, wide, wide), BF16)
    halves = pl.pallas_call(
        functools.partial(half_kernel, chunks),
        out_shape=[half_shape] * 4,
        in_specs=[SMEM] * 2 + [VMEM] * 3,
        out_specs=[VMEM] * 4,
        name="half",
        **options,
    )(block_list, rows, by_mu(three_centre), other, expanded)
    for distances in rounds[1:-1]:
        arrived = [flip(virt, distance, count) for distance in distances]
        virt = jnp.stack([virt] + arrived, axis=1).reshape((-1,) + virt.shape[1:])
    arrived = [virt] + [flip(virt, distance, count) for distance in rounds[-1]]
    arrived[:2], halves = lax.optimization_barrier((arrived[:2], halves))
    early = jnp.stack(arrived[:all_turns // 2])
    places = count // 2
    total_shape = (16, places * groups_dev)
    total = pl.pallas_call(
        functools.partial(early_kernel, chunks),
        out_shape=jax.ShapeDtypeStruct(total_shape, F32),
        in_specs=[SMEM] * 3 + [VMEM] * 3,
        out_specs=VMEM,
        name="early",
        **options,
    )(block_list, slots, owners, *halves[:2], early)
    arrived, total = lax.optimization_barrier((arrived[all_turns // 2:], total))
    partial = pl.pallas_call(
        functools.partial(late_kernel, scale, chunks),
        out_shape=jax.ShapeDtypeStruct((2 * count, 8 * groups_dev), F32),
        in_specs=[SMEM] * 3 + [VMEM] * 4,
        out_specs=VMEM,
        scratch_shapes=[pltpu.VMEM(total_shape, F32)],
        name="late",
        **options,
    )(block_list, slots, owners, *halves[2:], jnp.stack(arrived), total)

    arrived = lax.all_to_all(partial, ("blk", "aux"), 0, 0, tiled=True)
    return jnp.sum(arrived, axis=0).reshape(2, 4, groups_dev).transpose(2, 0, 1)


def solution(mesh):
    in_specs = (
        P("blk", "aux", None),
        P("blk", None, None),
        P("blk", None, None),
        P("blk"),
        P("blk"),
        P("blk", None),
    )
    out_specs = P("blk", "aux", None)
    return jax.shard_map(
        functools.partial(body, mesh.shape["blk"]),
        mesh=mesh,
        in_specs=in_specs,
        out_specs=out_specs,
        check_vma=False,
    )
```

time: 34.5 us -> 34.1 us (0.988)
  blocking collectives: 11.3 us -> 12.7 us
  Pallas kernels: 8.02 us -> 7.04 us
  waiting for transfers between devices: 3.77 us -> 3.13 us
  local copies, waits for them, and re-layouts: 1.61 us -> 1.15 us
  starting transfers between devices: 9.32 us -> 9.77 us
    ppermute x2, waiting for transfers between devices: 2.27 us -> 0.01 us  [split_flip(): return lax.ppermute(values, ('blk', 'aux'), pairs)]
    ppermute x3, waiting for transfers between devices: 1.5 us -> 3.12 us  [flip(): lax.ppermute(values, 'blk', [(i, i ^ distance) for i in range(count)])]
    all_to_all x1, blocking collectives: 11.3 us -> 12.7 us  [body(): arrived = lax.all_to_all(partial, ('blk', 'aux'), 0, 0, tiled=True)]
    pallas_call x2 -> x4, Pallas kernels: 8.02 us -> 7.04 us  [the longest x1 1.92 us: body(): pl.pallas_call(functools.partial(half_kernel, chunks), out_shape=[half_sh...]
    slice x1 -> x0, local copies, waits for them, and re-layouts: 0.88 us -> none  [body(): virt = jnp.concatenate([virtual_blocks[0::2], virtual_blocks[1::2]], axis=2)]
    unnamed x0 -> x4, local copies, waits for them, and re-layouts: none -> 0.46 us
    ppermute x2, starting transfers between devices: 5.32 us -> 5.77 us  [split_flip(): return lax.ppermute(values, ('blk', 'aux'), pairs)]
  transfers between devices with their start and end apart: 6 -> 6, of which waited for: 3 -> 3; matrix products, arithmetic and copies ran while one was open for 3% -> 0% of each run, Pallas kernels for 15% -> 16%
where the time goes in v1:
time: 34.1 us
  blocking collectives  12.7 us (37%)
  starting transfers between devices  9.77 us (29%)
  Pallas kernels  7.04 us (21%)
  waiting for transfers between devices  3.13 us (9%)
  local copies, waits for them, and re-layouts  1.15 us (3%)
    all_to_all x1, blocking collectives, body(): arrived = lax.all_to_all(partial, ('blk', 'aux'), 0, 0, tiled=True)  12.7 us
    ppermute x2, starting transfers between devices, split_flip(): return lax.ppermute(values, ('blk', 'aux'), pairs)  5.77 us
    ppermute x3, starting transfers between devices, flip(): lax.ppermute(values, 'blk', [(i, i ^ distance) for i in range(count)])  3.55 us
    ppermute x3, waiting for transfers between devices, flip(): lax.ppermute(values, 'blk', [(i, i ^ distance) for i in range(count)])  3.12 us
    pallas_call x1, Pallas kernels, body(): pl.pallas_call(functools.partial(half_kernel, chunks), out_shape=[half_sh...  1.92 us
    pallas_call x1, Pallas kernels, body(): pl.pallas_call(functools.partial(ready_kernel, count, bits_of(all_turns)...  1.79 us
    pallas_call x1, Pallas kernels, body(): pl.pallas_call(functools.partial(early_kernel, chunks), out_shape=jax.Sha...  1.68 us
    pallas_call x1, Pallas kernels, body(): pl.pallas_call(functools.partial(late_kernel, scale, chunks), out_shape=j...  1.64 us
  transfers between devices with their start and end apart: 6, of which 3 were waited for; matrix products, arithmetic and copies ran while one was open for 0% of the time, Pallas kernels for 16%

profile of v1, /device:TPU:0, one launch (start us, length us, event | category | flops | bytes accessed | tf_op | source)
XLA Modules:
  0.0 34.1 jit_solution(15278138302090211031)
XLA Ops:
  0.0 0.0 copy-start
  0.0 0.5 %collective-permute-start.3 = (bf16[128,64,128]{2,1,0:T(8,128)(2,1)}, bf16[128,64,128]{2,1,0:T(8,128)(2,1)S(1)}, u32[]{:S(2)}, u32[]{:S(2)}) collective-permute-start(bf16[128,64,128]{2,1,0:T(8,128)(2,1)} %bitcast.16), channel_id=1, source_target_pairs={{0,1},{1,0},{2,3},{3,2},{4,5},{5,4},{6,7},{7,6},{8,9},{9,8},{10,11... | collective-permute-start | bytes 6291464 | tf_op jit(solution)/shard_map/ppermute | solution.py:32
  0.5 0.4 %copy-done = bf16[8,64,64]{2,1,0:T(8,128)(2,1)S(1)} copy-done((bf16[8,64,64]{2,1,0:T(8,128)(2,1)S(1)}, bf16[8,64,64]{2,1,0:T(8,128)(2,1)}, u32[]{:S(2)}) %copy-start) | copy-done | bytes 65560
  0.9 0.0 copy-start.1
  0.9 0.1 pad_maximum_fusion.3
  1.0 5.1 %collective-permute-start = (bf16[4,64,128]{2,1,0:T(8,128)(2,1)S(1)}, bf16[4,64,128]{2,1,0:T(8,128)(2,1)S(1)}, u32[]{:S(2)}, u32[]{:S(2)}) collective-permute-start(bf16[4,64,128]{2,1,0:T(8,128)(2,1)S(1)} %pad_maximum_fusion.3), channel_id=1, source_target_pairs={{0,24},{1,9},{2,26},{3,11},{4,28},{5,13},{6,30},{7,15},{8,16},{9,1... | collective-permute-start | bytes 196616 | tf_op jit(solution)/shard_map/ppermute | solution.py:37
  6.1 0.7 %collective-permute-start.1 = (bf16[4,64,128]{2,1,0:T(8,128)(2,1)S(1)}, bf16[4,64,128]{2,1,0:T(8,128)(2,1)S(1)}, u32[]{:S(2)}, u32[]{:S(2)}) collective-permute-start(bf16[4,64,128]{2,1,0:T(8,128)(2,1)S(1)} %pad_maximum_fusion.3), channel_id=1, source_target_pairs={{0,0},{1,17},{2,2},{3,19},{4,4},{5,21},{6,6},{7,23},{8,8},{9,25},{... | collective-permute-start | bytes 196616 | tf_op jit(solution)/shard_map/ppermute | solution.py:37
  6.8 1.8 %ready.1 = (bf16[8,128,128]{2,1,0:T(8,128)(2,1)S(1)}, s32[258]{0:T(512)S(4)}, s32[128]{0:T(128)S(4)}, s32[128]{0:T(128)S(4)}, s32[128]{0:T(128)S(4)}) custom-call(s32[128]{0:T(128)} %rows_ref.1, s32[128]{0:T(128)} %slots_ref.1, s32[128]{0:T(128)} %bitcast.25, bf16[8,64,64]{2,1,0:T(8,128)(2,1)} %occ_ref.1), custom_call_target="tpu_custom_call" | custom-call | flops 1000000000 | bytes 4194304 | tf_op jit(solution)/shard_map/ready/pallas_call | solution.py:264
  8.6 0.0 collective-permute-done
  8.6 0.0 collective-permute-done.1
  8.6 1.6 %collective-permute-start.2 = (bf16[2,4,64,128]{3,2,1,0:T(8,128)(2,1)S(1)}, bf16[2,4,64,128]{3,2,1,0:T(8,128)(2,1)S(1)}, u32[]{:S(2)}, u32[]{:S(2)}) collective-permute-start(bf16[2,4,64,128]{3,2,1,0:T(8,128)(2,1)S(1)} %pad_maximum_fusion.2), channel_id=1, source_target_pairs={{0,2},{2,0},{4,6},{6,4},{8,10},{10,8},{12,14},{14,12},{16,18},{18,... | collective-permute-start | bytes 393224 | tf_op jit(solution)/shard_map/ppermute | solution.py:28
  10.2 1.5 %collective-permute-start.4 = (bf16[2,4,64,128]{3,2,1,0:T(8,128)(2,1)S(1)}, bf16[2,4,64,128]{3,2,1,0:T(8,128)(2,1)S(1)}, u32[]{:S(2)}, u32[]{:S(2)}) collective-permute-start(bf16[2,4,64,128]{3,2,1,0:T(8,128)(2,1)S(1)} %pad_maximum_fusion.2), channel_id=1, source_target_pairs={{0,4},{2,6},{4,0},{6,2},{8,12},{10,14},{12,8},{14,10},{16,20},{18,... | collective-permute-start | bytes 393224 | tf_op jit(solution)/shard_map/ppermute | solution.py:28
  11.7 0.5 %collective-permute-start.5 = (bf16[2,4,64,128]{3,2,1,0:T(8,128)(2,1)S(1)}, bf16[2,4,64,128]{3,2,1,0:T(8,128)(2,1)S(1)}, u32[]{:S(2)}, u32[]{:S(2)}) collective-permute-start(bf16[2,4,64,128]{3,2,1,0:T(8,128)(2,1)S(1)} %pad_maximum_fusion.2), channel_id=1, source_target_pairs={{0,6},{2,4},{4,2},{6,0},{8,14},{10,12},{12,10},{14,8},{16,22},{18,... | collective-permute-start | bytes 393224 | tf_op jit(solution)/shard_map/ppermute | solution.py:28
  12.2 0.0 collective-permute-done.3.other_ref
  12.2 0.0 copy-done.1
  12.2 1.9 %half.1 = (bf16[64,128,128]{2,1,0:T(8,128)(2,1)S(1)}, bf16[64,128,128]{2,1,0:T(8,128)(2,1)S(1)}, bf16[64,128,128]{2,1,0:T(8,128)(2,1)S(1)}, bf16[64,128,128]{2,1,0:T(8,128)(2,1)S(1)}) custom-call(s32[258]{0:T(512)S(4)} %get-tuple-element.28.list_ref, s32[128]{0:T(128)S(4)} %get-tuple-element.36.rows, bf16[128,64,128]{2,1,0:T(8,128)(2,1)S(1)} %bitcast.17, ...), custom_call_target="tpu_custom_call" | custom-call | flops 1000000000 | bytes 4194304 | tf_op jit(solution)/shard_map/half/pallas_call | solution.py:282
  14.1 0.3 %collective-permute-done.2 = bf16[2,4,64,128]{3,2,1,0:T(8,128)(2,1)S(1)} collective-permute-done((bf16[2,4,64,128]{3,2,1,0:T(8,128)(2,1)S(1)}, bf16[2,4,64,128]{3,2,1,0:T(8,128)(2,1)S(1)}, u32[]{:S(2)}, u32[]{:S(2)}) %collective-permute-start.2) | collective-permute-done | bytes 131104 | tf_op jit(solution)/shard_map/ppermute | solution.py:28
  14.5 1.7 %early.1.early_ref = f32[16,64]{1,0:T(8,128)S(1)} custom-call(s32[258]{0:T(512)S(4)} %get-tuple-element.28.list_ref, s32[128]{0:T(128)S(4)} %get-tuple-element.29.slots, s32[128]{0:T(128)S(4)} %get-tuple-element.30.owners, bf16[64,128,128]{2,1,0:T(8,128)(2,1)S(1)} %get-tuple-element.44.own_ref, bf16[64,128,128]{2,1,0:T(8,128)(2,1)S(1)} %get-tuple-element.45.other_ref, ...), custom_call_target="tpu_custom_call" | custom-call | flops 1000000000 | bytes 4194304 | tf_op jit(solution)/shard_map/early/pallas_call | solution.py:298
  16.2 1.9 %collective-permute-done.4 = bf16[2,4,64,128]{3,2,1,0:T(8,128)(2,1)S(1)} collective-permute-done((bf16[2,4,64,128]{3,2,1,0:T(8,128)(2,1)S(1)}, bf16[2,4,64,128]{3,2,1,0:T(8,128)(2,1)S(1)}, u32[]{:S(2)}, u32[]{:S(2)}) %collective-permute-start.4) | collective-permute-done | bytes 131104 | tf_op jit(solution)/shard_map/ppermute | solution.py:28
  18.1 0.9 %collective-permute-done.5 = bf16[2,4,64,128]{3,2,1,0:T(8,128)(2,1)S(1)} collective-permute-done((bf16[2,4,64,128]{3,2,1,0:T(8,128)(2,1)S(1)}, bf16[2,4,64,128]{3,2,1,0:T(8,128)(2,1)S(1)}, u32[]{:S(2)}, u32[]{:S(2)}) %collective-permute-start.5) | collective-permute-done | bytes 131104 | tf_op jit(solution)/shard_map/ppermute | solution.py:28
  19.0 1.6 %late.1 = f32[32,64]{1,0:T(8,128)S(1)} custom-call(s32[258]{0:T(512)S(4)} %get-tuple-element.28.list_ref, s32[128]{0:T(128)S(4)} %get-tuple-element.29.slots, s32[128]{0:T(128)S(4)} %get-tuple-element.30.owners, bf16[64,128,128]{2,1,0:T(8,128)(2,1)S(1)} %get-tuple-element.42.own_ref, bf16[64,128,128]{2,1,0:T(8,128)(2,1)S(1)} %get-tuple-element.43.other_ref, ...), custom_call_target="tpu_custom_call" | custom-call | flops 1000000000 | bytes 4194304 | tf_op jit(solution)/shard_map/late/pallas_call | solution.py:307
  20.7 12.7 %all_to_all.9 = f32[32,1,64]{2,1,0:T(1,128)S(1)} all-to-all(f32[32,1,64]{2,1,0:T(1,128)S(1)} %bitcast.18), channel_id=1, replica_groups=mesh['blk'=16,'aux'=2] {'blk','aux'}, dimensions={0} | all-to-all | bytes 16384 | tf_op jit(solution)/shard_map/all_to_all | solution.py:317
  33.3 0.1 reduce_sum.9
  33.4 0.7 %reshape.19 = f32[2,4,8]{2,1,0:T(4,128)} reshape(f32[64]{0:T(128)S(1)} %reduce_sum.9) | data formatting | bytes 512 | tf_op jit(solution)/shard_map/reshape | solution.py:318
  (5 shorter events, 0.1 us)
Async XLA Ops:
  0.0 0.9 %copy-start = (bf16[8,64,64]{2,1,0:T(8,128)(2,1)S(1)}, bf16[8,64,64]{2,1,0:T(8,128)(2,1)}, u32[]{:S(2)}) copy-start(bf16[8,64,64]{2,1,0:T(8,128)(2,1)} %param.8) | copy-start | bytes 196612
  0.0 12.2 %collective-permute-start.3 = (bf16[128,64,128]{2,1,0:T(8,128)(2,1)}, bf16[128,64,128]{2,1,0:T(8,128)(2,1)S(1)}, u32[]{:S(2)}, u32[]{:S(2)}) collective-permute-start(bf16[128,64,128]{2,1,0:T(8,128)(2,1)} %bitcast.16), channel_id=1, source_target_pairs={{0,1},{1,0},{2,3},{3,2},{4,5},{5,4},{6,7},{7,6},{8,9},{9,8},{10,11... | collective-permute-start | bytes 6291464 | tf_op jit(solution)/shard_map/ppermute | solution.py:32
  0.9 11.3 %copy-start.1 = (bf16[128,2,4096]{2,1,0:T(2,128)(2,1)S(1)}, bf16[128,2,4096]{2,1,0:T(2,128)(2,1)}, u32[]{:S(2)}) copy-start(bf16[128,2,4096]{2,1,0:T(2,128)(2,1)} %param.6) | copy-start | bytes 6291460
  1.0 7.6 %collective-permute-start = (bf16[4,64,128]{2,1,0:T(8,128)(2,1)S(1)}, bf16[4,64,128]{2,1,0:T(8,128)(2,1)S(1)}, u32[]{:S(2)}, u32[]{:S(2)}) collective-permute-start(bf16[4,64,128]{2,1,0:T(8,128)(2,1)S(1)} %pad_maximum_fusion.3), channel_id=1, source_target_pairs={{0,24},{1,9},{2,26},{3,11},{4,28},{5,13},{6,30},{7,15},{8,16},{9,1... | collective-permute-start | bytes 196616 | tf_op jit(solution)/shard_map/ppermute | solution.py:37
  6.1 2.5 %collective-permute-start.1 = (bf16[4,64,128]{2,1,0:T(8,128)(2,1)S(1)}, bf16[4,64,128]{2,1,0:T(8,128)(2,1)S(1)}, u32[]{:S(2)}, u32[]{:S(2)}) collective-permute-start(bf16[4,64,128]{2,1,0:T(8,128)(2,1)S(1)} %pad_maximum_fusion.3), channel_id=1, source_target_pairs={{0,0},{1,17},{2,2},{3,19},{4,4},{5,21},{6,6},{7,23},{8,8},{9,25},{... | collective-permute-start | bytes 196616 | tf_op jit(solution)/shard_map/ppermute | solution.py:37
  8.6 5.8 %collective-permute-start.2 = (bf16[2,4,64,128]{3,2,1,0:T(8,128)(2,1)S(1)}, bf16[2,4,64,128]{3,2,1,0:T(8,128)(2,1)S(1)}, u32[]{:S(2)}, u32[]{:S(2)}) collective-permute-start(bf16[2,4,64,128]{3,2,1,0:T(8,128)(2,1)S(1)} %pad_maximum_fusion.2), channel_id=1, source_target_pairs={{0,2},{2,0},{4,6},{6,4},{8,10},{10,8},{12,14},{14,12},{16,18},{18,... | collective-permute-start | bytes 393224 | tf_op jit(solution)/shard_map/ppermute | solution.py:28
  10.2 7.9 %collective-permute-start.4 = (bf16[2,4,64,128]{3,2,1,0:T(8,128)(2,1)S(1)}, bf16[2,4,64,128]{3,2,1,0:T(8,128)(2,1)S(1)}, u32[]{:S(2)}, u32[]{:S(2)}) collective-permute-start(bf16[2,4,64,128]{3,2,1,0:T(8,128)(2,1)S(1)} %pad_maximum_fusion.2), channel_id=1, source_target_pairs={{0,4},{2,6},{4,0},{6,2},{8,12},{10,14},{12,8},{14,10},{16,20},{18,... | collective-permute-start | bytes 393224 | tf_op jit(solution)/shard_map/ppermute | solution.py:28
  11.7 7.3 %collective-permute-start.5 = (bf16[2,4,64,128]{3,2,1,0:T(8,128)(2,1)S(1)}, bf16[2,4,64,128]{3,2,1,0:T(8,128)(2,1)S(1)}, u32[]{:S(2)}, u32[]{:S(2)}) collective-permute-start(bf16[2,4,64,128]{3,2,1,0:T(8,128)(2,1)S(1)} %pad_maximum_fusion.2), channel_id=1, source_target_pairs={{0,6},{2,4},{4,2},{6,0},{8,14},{10,12},{12,10},{14,8},{16,22},{18,... | collective-permute-start | bytes 393224 | tf_op jit(solution)/shard_map/ppermute | solution.py:28

commit v2 on v1

--- a/solution.py
+++ b/solution.py
@@ -65,7 +65,7 @@
     def add(block, found):
         early, late = found
         away = owners[block] ^ me
-        mine = (((away + quarter) >> (bits_of(quarter) + 1)) & 1) ^ core
+        mine = (away >> (bits_of(quarter) + 1)) ^ (1 - core)
         late_here = mine & (away >> late_bit)
         list_ref[jnp.where((away >> late_bit) & 1 == 1, late, early)] = block
         return early + mine - late_here, late + late_here
@@ -226,7 +226,7 @@
             for index in range(8):
                 place = start + index
                 second = place // quarter
-                far = jnp.where(core == 0, 3 - 3 * second, 1 + second)
+                far = 2 * core + 1 - second
                 owner = me ^ (far * quarter + place % quarter)
                 out_ref[pl.ds(2 * owner + target, 1), :] = turned[index:index + 1, :rows]
 
@@ -254,7 +254,7 @@
     left, whole = lax.optimization_barrier((left, virtual_blocks))
     virt = jnp.concatenate([left, lax.dynamic_slice_in_dim(whole, (1 - core) * tiles, tiles)], axis=2)
     other = swap_cores(by_mu(three_centre))
-    arrived = [split_flip(virt, far, near, count), split_flip(virt, 0, mid, count)]
+    arrived = [split_flip(virt, near, far, count), split_flip(virt, 0, mid, count)]
     integers = pltpu.SMEM((block_count,), jnp.int32)
     options = dict(
         compiler_params=pltpu.CompilerParams(vmem_limit_bytes=16 * 1024 * 1024),

time: 34.1 us -> 32.1 us (0.941); the launches traced: 34.1 us -> 31.6 us
  starting transfers between devices: 9.77 us -> 7.75 us
  waiting for transfers between devices: 3.13 us -> 2.61 us
    ppermute x2, starting transfers between devices: 5.77 us -> 3.74 us  [split_flip(): return lax.ppermute(values, ('blk', 'aux'), pairs)]
    ppermute x3, waiting for transfers between devices: 3.12 us -> 2.6 us  [flip(): lax.ppermute(values, 'blk', [(i, i ^ distance) for i in range(count)])]
  transfers between devices with their start and end apart: 6 -> 6, of which waited for: 3 -> 1; matrix products, arithmetic and copies ran while one was open for 0% -> 0% of each run, Pallas kernels for 16% -> 17%
where the time goes in v2:
time: 32.1 us; the launch traced here: 31.6 us
  blocking collectives  12.9 us (40%)
  starting transfers between devices  7.75 us (24%)
  Pallas kernels  6.92 us (22%)
  waiting for transfers between devices  2.61 us (8%)
  local copies, waits for them, and re-layouts  1.15 us (4%)
    all_to_all x1, blocking collectives, body(): arrived = lax.all_to_all(partial, ('blk', 'aux'), 0, 0, tiled=True)  12.9 us
    ppermute x2, starting transfers between devices, split_flip(): return lax.ppermute(values, ('blk', 'aux'), pairs)  3.74 us
    ppermute x3, starting transfers between devices, flip(): lax.ppermute(values, 'blk', [(i, i ^ distance) for i in range(count)])  3.55 us
    ppermute x3, waiting for transfers between devices, flip(): lax.ppermute(values, 'blk', [(i, i ^ distance) for i in range(count)])  2.6 us
    pallas_call x1, Pallas kernels, body(): pl.pallas_call(functools.partial(half_kernel, chunks), out_shape=[half_sh...  1.91 us
    pallas_call x1, Pallas kernels, body(): pl.pallas_call(functools.partial(ready_kernel, count, bits_of(all_turns)...  1.69 us
    pallas_call x1, Pallas kernels, body(): pl.pallas_call(functools.partial(early_kernel, chunks), out_shape=jax.Sha...  1.68 us
    pallas_call x1, Pallas kernels, body(): pl.pallas_call(functools.partial(late_kernel, scale, chunks), out_shape=j...  1.64 us
  transfers between devices with their start and end apart: 6, of which 1 were waited for; matrix products, arithmetic and copies ran while one was open for 0% of the time, Pallas kernels for 17%

profile of v2, /device:TPU:0, one launch (start us, length us, event | category | flops | bytes accessed | tf_op | source)
XLA Modules:
  0.0 31.6 jit_solution(11480703483585165171)
XLA Ops:
  0.0 0.0 copy-start
  0.0 0.5 %collective-permute-start.3 = (bf16[128,64,128]{2,1,0:T(8,128)(2,1)}, bf16[128,64,128]{2,1,0:T(8,128)(2,1)S(1)}, u32[]{:S(2)}, u32[]{:S(2)}) collective-permute-start(bf16[128,64,128]{2,1,0:T(8,128)(2,1)} %bitcast.16), channel_id=1, source_target_pairs={{0,1},{1,0},{2,3},{3,2},{4,5},{5,4},{6,7},{7,6},{8,9},{9,8},{10,11... | collective-permute-start | bytes 6291464 | tf_op jit(solution)/shard_map/ppermute | solution.py:32
  0.5 0.4 %copy-done = bf16[8,64,64]{2,1,0:T(8,128)(2,1)S(1)} copy-done((bf16[8,64,64]{2,1,0:T(8,128)(2,1)S(1)}, bf16[8,64,64]{2,1,0:T(8,128)(2,1)}, u32[]{:S(2)}) %copy-start) | copy-done | bytes 65560
  0.9 0.0 copy-start.1
  0.9 0.1 pad_maximum_fusion.3
  1.0 3.1 %collective-permute-start = (bf16[4,64,128]{2,1,0:T(8,128)(2,1)S(1)}, bf16[4,64,128]{2,1,0:T(8,128)(2,1)S(1)}, u32[]{:S(2)}, u32[]{:S(2)}) collective-permute-start(bf16[4,64,128]{2,1,0:T(8,128)(2,1)S(1)} %pad_maximum_fusion.3), channel_id=1, source_target_pairs={{0,8},{1,25},{2,10},{3,27},{4,12},{5,29},{6,14},{7,31},{8,0},{9,17... | collective-permute-start | bytes 196616 | tf_op jit(solution)/shard_map/ppermute | solution.py:37
  4.1 0.7 %collective-permute-start.1 = (bf16[4,64,128]{2,1,0:T(8,128)(2,1)S(1)}, bf16[4,64,128]{2,1,0:T(8,128)(2,1)S(1)}, u32[]{:S(2)}, u32[]{:S(2)}) collective-permute-start(bf16[4,64,128]{2,1,0:T(8,128)(2,1)S(1)} %pad_maximum_fusion.3), channel_id=1, source_target_pairs={{0,0},{1,17},{2,2},{3,19},{4,4},{5,21},{6,6},{7,23},{8,8},{9,25},{... | collective-permute-start | bytes 196616 | tf_op jit(solution)/shard_map/ppermute | solution.py:37
  4.8 1.7 %ready.1 = (bf16[8,128,128]{2,1,0:T(8,128)(2,1)S(1)}, s32[258]{0:T(512)S(4)}, s32[128]{0:T(128)S(4)}, s32[128]{0:T(128)S(4)}, s32[128]{0:T(128)S(4)}) custom-call(s32[128]{0:T(128)} %rows_ref.1, s32[128]{0:T(128)} %slots_ref.1, s32[128]{0:T(128)} %bitcast.25, bf16[8,64,64]{2,1,0:T(8,128)(2,1)} %occ_ref.1), custom_call_target="tpu_custom_call" | custom-call | flops 1000000000 | bytes 4194304 | tf_op jit(solution)/shard_map/ready/pallas_call | solution.py:264
  6.5 0.0 collective-permute-done
  6.5 0.0 collective-permute-done.1
  6.5 1.9 %collective-permute-start.2 = (bf16[2,4,64,128]{3,2,1,0:T(8,128)(2,1)S(1)}, bf16[2,4,64,128]{3,2,1,0:T(8,128)(2,1)S(1)}, u32[]{:S(2)}, u32[]{:S(2)}) collective-permute-start(bf16[2,4,64,128]{3,2,1,0:T(8,128)(2,1)S(1)} %pad_maximum_fusion.2), channel_id=1, source_target_pairs={{0,2},{2,0},{4,6},{6,4},{8,10},{10,8},{12,14},{14,12},{16,18},{18,... | collective-permute-start | bytes 393224 | tf_op jit(solution)/shard_map/ppermute | solution.py:28
  8.4 1.5 %collective-permute-start.4 = (bf16[2,4,64,128]{3,2,1,0:T(8,128)(2,1)S(1)}, bf16[2,4,64,128]{3,2,1,0:T(8,128)(2,1)S(1)}, u32[]{:S(2)}, u32[]{:S(2)}) collective-permute-start(bf16[2,4,64,128]{3,2,1,0:T(8,128)(2,1)S(1)} %pad_maximum_fusion.2), channel_id=1, source_target_pairs={{0,4},{2,6},{4,0},{6,2},{8,12},{10,14},{12,8},{14,10},{16,20},{18,... | collective-permute-start | bytes 393224 | tf_op jit(solution)/shard_map/ppermute | solution.py:28
  9.9 0.2 collective-permute-start.5
  10.1 0.0 collective-permute-done.3.other_ref
  10.1 0.0 copy-done.1
  10.1 1.9 %half.1 = (bf16[64,128,128]{2,1,0:T(8,128)(2,1)S(1)}, bf16[64,128,128]{2,1,0:T(8,128)(2,1)S(1)}, bf16[64,128,128]{2,1,0:T(8,128)(2,1)S(1)}, bf16[64,128,128]{2,1,0:T(8,128)(2,1)S(1)}) custom-call(s32[258]{0:T(512)S(4)} %get-tuple-element.28.list_ref, s32[128]{0:T(128)S(4)} %get-tuple-element.36.rows, bf16[128,64,128]{2,1,0:T(8,128)(2,1)S(1)} %bitcast.17, ...), custom_call_target="tpu_custom_call" | custom-call | flops 1000000000 | bytes 4194304 | tf_op jit(solution)/shard_map/half/pallas_call | solution.py:282
  12.0 0.0 collective-permute-done.2
  12.0 1.7 %early.1.early_ref = f32[16,64]{1,0:T(8,128)S(1)} custom-call(s32[258]{0:T(512)S(4)} %get-tuple-element.28.list_ref, s32[128]{0:T(128)S(4)} %get-tuple-element.29.slots, s32[128]{0:T(128)S(4)} %get-tuple-element.30.owners, bf16[64,128,128]{2,1,0:T(8,128)(2,1)S(1)} %get-tuple-element.44.own_ref, bf16[64,128,128]{2,1,0:T(8,128)(2,1)S(1)} %get-tuple-element.45.other_ref, ...), custom_call_target="tpu_custom_call" | custom-call | flops 1000000000 | bytes 4194304 | tf_op jit(solution)/shard_map/early/pallas_call | solution.py:298
  13.7 0.0 collective-permute-done.4
  13.7 2.6 %collective-permute-done.5 = bf16[2,4,64,128]{3,2,1,0:T(8,128)(2,1)S(1)} collective-permute-done((bf16[2,4,64,128]{3,2,1,0:T(8,128)(2,1)S(1)}, bf16[2,4,64,128]{3,2,1,0:T(8,128)(2,1)S(1)}, u32[]{:S(2)}, u32[]{:S(2)}) %collective-permute-start.5) | collective-permute-done | bytes 131104 | tf_op jit(solution)/shard_map/ppermute | solution.py:28
  16.4 1.6 %late.1 = f32[32,64]{1,0:T(8,128)S(1)} custom-call(s32[258]{0:T(512)S(4)} %get-tuple-element.28.list_ref, s32[128]{0:T(128)S(4)} %get-tuple-element.29.slots, s32[128]{0:T(128)S(4)} %get-tuple-element.30.owners, bf16[64,128,128]{2,1,0:T(8,128)(2,1)S(1)} %get-tuple-element.42.own_ref, bf16[64,128,128]{2,1,0:T(8,128)(2,1)S(1)} %get-tuple-element.43.other_ref, ...), custom_call_target="tpu_custom_call" | custom-call | flops 1000000000 | bytes 4194304 | tf_op jit(solution)/shard_map/late/pallas_call | solution.py:307
  18.0 12.9 %all_to_all.9 = f32[32,1,64]{2,1,0:T(1,128)S(1)} all-to-all(f32[32,1,64]{2,1,0:T(1,128)S(1)} %bitcast.18), channel_id=1, replica_groups=mesh['blk'=16,'aux'=2] {'blk','aux'}, dimensions={0} | all-to-all | bytes 16384 | tf_op jit(solution)/shard_map/all_to_all | solution.py:317
  30.9 0.1 reduce_sum.9
  30.9 0.7 %reshape.19 = f32[2,4,8]{2,1,0:T(4,128)} reshape(f32[64]{0:T(128)S(1)} %reduce_sum.9) | data formatting | bytes 512 | tf_op jit(solution)/shard_map/reshape | solution.py:318
  (5 shorter events, 0.1 us)
Async XLA Ops:
  0.0 0.9 %copy-start = (bf16[8,64,64]{2,1,0:T(8,128)(2,1)S(1)}, bf16[8,64,64]{2,1,0:T(8,128)(2,1)}, u32[]{:S(2)}) copy-start(bf16[8,64,64]{2,1,0:T(8,128)(2,1)} %param.8) | copy-start | bytes 196612
  0.0 10.1 %collective-permute-start.3 = (bf16[128,64,128]{2,1,0:T(8,128)(2,1)}, bf16[128,64,128]{2,1,0:T(8,128)(2,1)S(1)}, u32[]{:S(2)}, u32[]{:S(2)}) collective-permute-start(bf16[128,64,128]{2,1,0:T(8,128)(2,1)} %bitcast.16), channel_id=1, source_target_pairs={{0,1},{1,0},{2,3},{3,2},{4,5},{5,4},{6,7},{7,6},{8,9},{9,8},{10,11... | collective-permute-start | bytes 6291464 | tf_op jit(solution)/shard_map/ppermute | solution.py:32
  0.9 9.2 %copy-start.1 = (bf16[128,2,4096]{2,1,0:T(2,128)(2,1)S(1)}, bf16[128,2,4096]{2,1,0:T(2,128)(2,1)}, u32[]{:S(2)}) copy-start(bf16[128,2,4096]{2,1,0:T(2,128)(2,1)} %param.6) | copy-start | bytes 6291460
  1.0 5.4 %collective-permute-start = (bf16[4,64,128]{2,1,0:T(8,128)(2,1)S(1)}, bf16[4,64,128]{2,1,0:T(8,128)(2,1)S(1)}, u32[]{:S(2)}, u32[]{:S(2)}) collective-permute-start(bf16[4,64,128]{2,1,0:T(8,128)(2,1)S(1)} %pad_maximum_fusion.3), channel_id=1, source_target_pairs={{0,8},{1,25},{2,10},{3,27},{4,12},{5,29},{6,14},{7,31},{8,0},{9,17... | collective-permute-start | bytes 196616 | tf_op jit(solution)/shard_map/ppermute | solution.py:37
  4.1 2.4 %collective-permute-start.1 = (bf16[4,64,128]{2,1,0:T(8,128)(2,1)S(1)}, bf16[4,64,128]{2,1,0:T(8,128)(2,1)S(1)}, u32[]{:S(2)}, u32[]{:S(2)}) collective-permute-start(bf16[4,64,128]{2,1,0:T(8,128)(2,1)S(1)} %pad_maximum_fusion.3), channel_id=1, source_target_pairs={{0,0},{1,17},{2,2},{3,19},{4,4},{5,21},{6,6},{7,23},{8,8},{9,25},{... | collective-permute-start | bytes 196616 | tf_op jit(solution)/shard_map/ppermute | solution.py:37
  6.5 5.5 %collective-permute-start.2 = (bf16[2,4,64,128]{3,2,1,0:T(8,128)(2,1)S(1)}, bf16[2,4,64,128]{3,2,1,0:T(8,128)(2,1)S(1)}, u32[]{:S(2)}, u32[]{:S(2)}) collective-permute-start(bf16[2,4,64,128]{3,2,1,0:T(8,128)(2,1)S(1)} %pad_maximum_fusion.2), channel_id=1, source_target_pairs={{0,2},{2,0},{4,6},{6,4},{8,10},{10,8},{12,14},{14,12},{16,18},{18,... | collective-permute-start | bytes 393224 | tf_op jit(solution)/shard_map/ppermute | solution.py:28
  8.4 5.3 %collective-permute-start.4 = (bf16[2,4,64,128]{3,2,1,0:T(8,128)(2,1)S(1)}, bf16[2,4,64,128]{3,2,1,0:T(8,128)(2,1)S(1)}, u32[]{:S(2)}, u32[]{:S(2)}) collective-permute-start(bf16[2,4,64,128]{3,2,1,0:T(8,128)(2,1)S(1)} %pad_maximum_fusion.2), channel_id=1, source_target_pairs={{0,4},{2,6},{4,0},{6,2},{8,12},{10,14},{12,8},{14,10},{16,20},{18,... | collective-permute-start | bytes 393224 | tf_op jit(solution)/shard_map/ppermute | solution.py:28
  9.9 6.4 %collective-permute-start.5 = (bf16[2,4,64,128]{3,2,1,0:T(8,128)(2,1)S(1)}, bf16[2,4,64,128]{3,2,1,0:T(8,128)(2,1)S(1)}, u32[]{:S(2)}, u32[]{:S(2)}) collective-permute-start(bf16[2,4,64,128]{3,2,1,0:T(8,128)(2,1)S(1)} %pad_maximum_fusion.2), channel_id=1, source_target_pairs={{0,6},{2,4},{4,2},{6,0},{8,14},{10,12},{12,10},{14,8},{16,22},{18,... | collective-permute-start | bytes 393224 | tf_op jit(solution)/shard_map/ppermute | solution.py:28

commit v3 on v2

--- a/solution.py
+++ b/solution.py
@@ -250,9 +250,7 @@
 
     chunks = (5 * pairs // 8,) + (pairs // 8,) * 3 + (pairs // 4,) * 4
     tiles = groups_dev // 2
-    left = lax.dynamic_slice_in_dim(virtual_blocks, core * tiles, tiles)
-    left, whole = lax.optimization_barrier((left, virtual_blocks))
-    virt = jnp.concatenate([left, lax.dynamic_slice_in_dim(whole, (1 - core) * tiles, tiles)], axis=2)
+    virt = jnp.concatenate([lax.dynamic_slice_in_dim(virtual_blocks, core * tiles, tiles), lax.dynamic_slice_in_dim(virtual_blocks, (1 - core) * tiles, tiles)], axis=2)
     other = swap_cores(by_mu(three_centre))
     arrived = [split_flip(virt, near, far, count), split_flip(virt, 0, mid, count)]
     integers = pltpu.SMEM((block_count,), jnp.int32)

time: 32.1 us -> 31.5 us (0.981)
  waiting for transfers between devices: 2.61 us -> 2.05 us
  starting transfers between devices: 7.75 us -> 7.3 us
  local copies, waits for them, and re-layouts: 1.15 us -> 1.57 us
    dynamic_slice x2 -> x1, local copies, waits for them, and re-layouts: 0.01 us -> 0.88 us  [body(): lax.dynamic_slice_in_dim(virtual_blocks, core * tiles, tiles)]
    ppermute x3, waiting for transfers between devices: 2.6 us -> 2.04 us  [flip(): lax.ppermute(values, 'blk', [(i, i ^ distance) for i in range(count)])]
    unnamed x4 -> x2, local copies, waits for them, and re-layouts: 0.46 us -> 0.01 us
    ppermute x2, starting transfers between devices: 3.74 us -> 3.29 us  [split_flip(): return lax.ppermute(values, ('blk', 'aux'), pairs)]
  transfers between devices with their start and end apart: 6 -> 6, of which waited for: 1 -> 1; matrix products, arithmetic and copies ran while one was open for 0% -> 3% of each run, Pallas kernels for 17% -> 17%
where the time goes in v3:
time: 31.5 us; the launch traced here: 31.3 us
  blocking collectives  13.1 us (42%)
  starting transfers between devices  7.3 us (23%)
  Pallas kernels  6.92 us (22%)
  waiting for transfers between devices  2.05 us (7%)
  local copies, waits for them, and re-layouts  1.57 us (5%)
    all_to_all x1, blocking collectives, body(): arrived = lax.all_to_all(partial, ('blk', 'aux'), 0, 0, tiled=True)  13.1 us
    ppermute x3, starting transfers between devices, flip(): lax.ppermute(values, 'blk', [(i, i ^ distance) for i in range(count)])  3.55 us
    ppermute x2, starting transfers between devices, split_flip(): return lax.ppermute(values, ('blk', 'aux'), pairs)  3.29 us
    ppermute x3, waiting for transfers between devices, flip(): lax.ppermute(values, 'blk', [(i, i ^ distance) for i in range(count)])  2.04 us
    pallas_call x1, Pallas kernels, body(): pl.pallas_call(functools.partial(half_kernel, chunks), out_shape=[half_sh...  1.91 us
    pallas_call x1, Pallas kernels, body(): pl.pallas_call(functools.partial(ready_kernel, count, bits_of(all_turns)...  1.69 us
    pallas_call x1, Pallas kernels, body(): pl.pallas_call(functools.partial(early_kernel, chunks), out_shape=jax.Sha...  1.68 us
    pallas_call x1, Pallas kernels, body(): pl.pallas_call(functools.partial(late_kernel, scale, chunks), out_shape=j...  1.64 us
  transfers between devices with their start and end apart: 6, of which 1 were waited for; matrix products, arithmetic and copies ran while one was open for 3% of the time, Pallas kernels for 17%

profile of v3, /device:TPU:0, one launch (start us, length us, event | category | flops | bytes accessed | tf_op | source)
XLA Modules:
  0.0 31.3 jit_solution(10583127577883047817)
XLA Ops:
  0.0 0.5 %collective-permute-start.3 = (bf16[128,64,128]{2,1,0:T(8,128)(2,1)}, bf16[128,64,128]{2,1,0:T(8,128)(2,1)S(1)}, u32[]{:S(2)}, u32[]{:S(2)}) collective-permute-start(bf16[128,64,128]{2,1,0:T(8,128)(2,1)} %bitcast.16), channel_id=1, source_target_pairs={{0,1},{1,0},{2,3},{3,2},{4,5},{5,4},{6,7},{7,6},{8,9},{9,8},{10,11... | collective-permute-start | bytes 6291464 | tf_op jit(solution)/shard_map/ppermute | solution.py:32
  0.5 0.9 %constant_dynamic-slice_fusion.1 = (bf16[4,64,64]{2,1,0:T(8,128)(2,1)S(1)}, bf16[4,64,64]{2,1,0:T(8,128)(2,1)S(1)}) fusion(bf16[8,64,64]{2,1,0:T(8,128)(2,1)} %param.8, s32[]{:T(128)S(6)} %select_n.6, s32[]{:T(128)S(6)} %select_n.7), kind=kLoop, calls=%fused_computation.5 | loop fusion | bytes 131080 | tf_op jit(solution)/shard_map/dynamic_slice | solution.py:253
  1.3 0.0 copy-start
  1.3 0.1 pad_maximum_fusion.3
  1.4 2.6 %collective-permute-start = (bf16[4,64,128]{2,1,0:T(8,128)(2,1)S(1)}, bf16[4,64,128]{2,1,0:T(8,128)(2,1)S(1)}, u32[]{:S(2)}, u32[]{:S(2)}) collective-permute-start(bf16[4,64,128]{2,1,0:T(8,128)(2,1)S(1)} %pad_maximum_fusion.3), channel_id=1, source_target_pairs={{0,8},{1,25},{2,10},{3,27},{4,12},{5,29},{6,14},{7,31},{8,0},{9,17... | collective-permute-start | bytes 196616 | tf_op jit(solution)/shard_map/ppermute | solution.py:37
  4.1 0.7 %collective-permute-start.1 = (bf16[4,64,128]{2,1,0:T(8,128)(2,1)S(1)}, bf16[4,64,128]{2,1,0:T(8,128)(2,1)S(1)}, u32[]{:S(2)}, u32[]{:S(2)}) collective-permute-start(bf16[4,64,128]{2,1,0:T(8,128)(2,1)S(1)} %pad_maximum_fusion.3), channel_id=1, source_target_pairs={{0,0},{1,17},{2,2},{3,19},{4,4},{5,21},{6,6},{7,23},{8,8},{9,25},{... | collective-permute-start | bytes 196616 | tf_op jit(solution)/shard_map/ppermute | solution.py:37
  4.7 1.7 %ready.1 = (bf16[8,128,128]{2,1,0:T(8,128)(2,1)S(1)}, s32[258]{0:T(512)S(4)}, s32[128]{0:T(128)S(4)}, s32[128]{0:T(128)S(4)}, s32[128]{0:T(128)S(4)}) custom-call(s32[128]{0:T(128)} %rows_ref.1, s32[128]{0:T(128)} %slots_ref.1, s32[128]{0:T(128)} %bitcast.25, bf16[8,64,64]{2,1,0:T(8,128)(2,1)} %occ_ref.1), custom_call_target="tpu_custom_call" | custom-call | flops 1000000000 | bytes 4194304 | tf_op jit(solution)/shard_map/ready/pallas_call | solution.py:262
  6.4 0.0 collective-permute-done
  6.5 0.0 collective-permute-done.1
  6.5 1.9 %collective-permute-start.2 = (bf16[2,4,64,128]{3,2,1,0:T(8,128)(2,1)S(1)}, bf16[2,4,64,128]{3,2,1,0:T(8,128)(2,1)S(1)}, u32[]{:S(2)}, u32[]{:S(2)}) collective-permute-start(bf16[2,4,64,128]{3,2,1,0:T(8,128)(2,1)S(1)} %pad_maximum_fusion.2), channel_id=1, source_target_pairs={{0,2},{2,0},{4,6},{6,4},{8,10},{10,8},{12,14},{14,12},{16,18},{18,... | collective-permute-start | bytes 393224 | tf_op jit(solution)/shard_map/ppermute | solution.py:28
  8.4 1.5 %collective-permute-start.4 = (bf16[2,4,64,128]{3,2,1,0:T(8,128)(2,1)S(1)}, bf16[2,4,64,128]{3,2,1,0:T(8,128)(2,1)S(1)}, u32[]{:S(2)}, u32[]{:S(2)}) collective-permute-start(bf16[2,4,64,128]{3,2,1,0:T(8,128)(2,1)S(1)} %pad_maximum_fusion.2), channel_id=1, source_target_pairs={{0,4},{2,6},{4,0},{6,2},{8,12},{10,14},{12,8},{14,10},{16,20},{18,... | collective-permute-start | bytes 393224 | tf_op jit(solution)/shard_map/ppermute | solution.py:28
  9.9 0.2 collective-permute-start.5
  10.0 0.0 collective-permute-done.3.other_ref
  10.0 0.0 copy-done
  10.0 1.9 %half.1 = (bf16[64,128,128]{2,1,0:T(8,128)(2,1)S(1)}, bf16[64,128,128]{2,1,0:T(8,128)(2,1)S(1)}, bf16[64,128,128]{2,1,0:T(8,128)(2,1)S(1)}, bf16[64,128,128]{2,1,0:T(8,128)(2,1)S(1)}) custom-call(s32[258]{0:T(512)S(4)} %get-tuple-element.26.list_ref, s32[128]{0:T(128)S(4)} %get-tuple-element.32.rows, bf16[128,64,128]{2,1,0:T(8,128)(2,1)S(1)} %bitcast.17, ...), custom_call_target="tpu_custom_call" | custom-call | flops 1000000000 | bytes 4194304 | tf_op jit(solution)/shard_map/half/pallas_call | solution.py:280
  12.0 0.0 collective-permute-done.2
  12.0 1.7 %early.1.early_ref = f32[16,64]{1,0:T(8,128)S(1)} custom-call(s32[258]{0:T(512)S(4)} %get-tuple-element.26.list_ref, s32[128]{0:T(128)S(4)} %get-tuple-element.27.slots, s32[128]{0:T(128)S(4)} %get-tuple-element.28.owners, bf16[64,128,128]{2,1,0:T(8,128)(2,1)S(1)} %get-tuple-element.40.own_ref, bf16[64,128,128]{2,1,0:T(8,128)(2,1)S(1)} %get-tuple-element.41.other_ref, ...), custom_call_target="tpu_custom_call" | custom-call | flops 1000000000 | bytes 4194304 | tf_op jit(solution)/shard_map/early/pallas_call | solution.py:296
  13.7 0.0 collective-permute-done.4
  13.7 2.0 %collective-permute-done.5 = bf16[2,4,64,128]{3,2,1,0:T(8,128)(2,1)S(1)} collective-permute-done((bf16[2,4,64,128]{3,2,1,0:T(8,128)(2,1)S(1)}, bf16[2,4,64,128]{3,2,1,0:T(8,128)(2,1)S(1)}, u32[]{:S(2)}, u32[]{:S(2)}) %collective-permute-start.5) | collective-permute-done | bytes 131104 | tf_op jit(solution)/shard_map/ppermute | solution.py:28
  15.8 1.6 %late.1 = f32[32,64]{1,0:T(8,128)S(1)} custom-call(s32[258]{0:T(512)S(4)} %get-tuple-element.26.list_ref, s32[128]{0:T(128)S(4)} %get-tuple-element.27.slots, s32[128]{0:T(128)S(4)} %get-tuple-element.28.owners, bf16[64,128,128]{2,1,0:T(8,128)(2,1)S(1)} %get-tuple-element.38.own_ref, bf16[64,128,128]{2,1,0:T(8,128)(2,1)S(1)} %get-tuple-element.39.other_ref, ...), custom_call_target="tpu_custom_call" | custom-call | flops 1000000000 | bytes 4194304 | tf_op jit(solution)/shard_map/late/pallas_call | solution.py:305
  17.4 13.1 %all_to_all.9 = f32[32,1,64]{2,1,0:T(1,128)S(1)} all-to-all(f32[32,1,64]{2,1,0:T(1,128)S(1)} %bitcast.18), channel_id=1, replica_groups=mesh['blk'=16,'aux'=2] {'blk','aux'}, dimensions={0} | all-to-all | bytes 16384 | tf_op jit(solution)/shard_map/all_to_all | solution.py:315
  30.5 0.1 reduce_sum.9
  30.6 0.7 %reshape.19 = f32[2,4,8]{2,1,0:T(4,128)} reshape(f32[64]{0:T(128)S(1)} %reduce_sum.9) | data formatting | bytes 512 | tf_op jit(solution)/shard_map/reshape | solution.py:316
  (3 shorter events, 0.1 us)
Async XLA Ops:
  0.0 10.0 %collective-permute-start.3 = (bf16[128,64,128]{2,1,0:T(8,128)(2,1)}, bf16[128,64,128]{2,1,0:T(8,128)(2,1)S(1)}, u32[]{:S(2)}, u32[]{:S(2)}) collective-permute-start(bf16[128,64,128]{2,1,0:T(8,128)(2,1)} %bitcast.16), channel_id=1, source_target_pairs={{0,1},{1,0},{2,3},{3,2},{4,5},{5,4},{6,7},{7,6},{8,9},{9,8},{10,11... | collective-permute-start | bytes 6291464 | tf_op jit(solution)/shard_map/ppermute | solution.py:32
  1.3 8.7 %copy-start = (bf16[128,2,4096]{2,1,0:T(2,128)(2,1)S(1)}, bf16[128,2,4096]{2,1,0:T(2,128)(2,1)}, u32[]{:S(2)}) copy-start(bf16[128,2,4096]{2,1,0:T(2,128)(2,1)} %param.6) | copy-start | bytes 6291460
  1.4 5.0 %collective-permute-start = (bf16[4,64,128]{2,1,0:T(8,128)(2,1)S(1)}, bf16[4,64,128]{2,1,0:T(8,128)(2,1)S(1)}, u32[]{:S(2)}, u32[]{:S(2)}) collective-permute-start(bf16[4,64,128]{2,1,0:T(8,128)(2,1)S(1)} %pad_maximum_fusion.3), channel_id=1, source_target_pairs={{0,8},{1,25},{2,10},{3,27},{4,12},{5,29},{6,14},{7,31},{8,0},{9,17... | collective-permute-start | bytes 196616 | tf_op jit(solution)/shard_map/ppermute | solution.py:37
  4.1 2.4 %collective-permute-start.1 = (bf16[4,64,128]{2,1,0:T(8,128)(2,1)S(1)}, bf16[4,64,128]{2,1,0:T(8,128)(2,1)S(1)}, u32[]{:S(2)}, u32[]{:S(2)}) collective-permute-start(bf16[4,64,128]{2,1,0:T(8,128)(2,1)S(1)} %pad_maximum_fusion.3), channel_id=1, source_target_pairs={{0,0},{1,17},{2,2},{3,19},{4,4},{5,21},{6,6},{7,23},{8,8},{9,25},{... | collective-permute-start | bytes 196616 | tf_op jit(solution)/shard_map/ppermute | solution.py:37
  6.5 5.5 %collective-permute-start.2 = (bf16[2,4,64,128]{3,2,1,0:T(8,128)(2,1)S(1)}, bf16[2,4,64,128]{3,2,1,0:T(8,128)(2,1)S(1)}, u32[]{:S(2)}, u32[]{:S(2)}) collective-permute-start(bf16[2,4,64,128]{3,2,1,0:T(8,128)(2,1)S(1)} %pad_maximum_fusion.2), channel_id=1, source_target_pairs={{0,2},{2,0},{4,6},{6,4},{8,10},{10,8},{12,14},{14,12},{16,18},{18,... | collective-permute-start | bytes 393224 | tf_op jit(solution)/shard_map/ppermute | solution.py:28
  8.4 5.3 %collective-permute-start.4 = (bf16[2,4,64,128]{3,2,1,0:T(8,128)(2,1)S(1)}, bf16[2,4,64,128]{3,2,1,0:T(8,128)(2,1)S(1)}, u32[]{:S(2)}, u32[]{:S(2)}) collective-permute-start(bf16[2,4,64,128]{3,2,1,0:T(8,128)(2,1)S(1)} %pad_maximum_fusion.2), channel_id=1, source_target_pairs={{0,4},{2,6},{4,0},{6,2},{8,12},{10,14},{12,8},{14,10},{16,20},{18,... | collective-permute-start | bytes 393224 | tf_op jit(solution)/shard_map/ppermute | solution.py:28
  9.9 5.9 %collective-permute-start.5 = (bf16[2,4,64,128]{3,2,1,0:T(8,128)(2,1)S(1)}, bf16[2,4,64,128]{3,2,1,0:T(8,128)(2,1)S(1)}, u32[]{:S(2)}, u32[]{:S(2)}) collective-permute-start(bf16[2,4,64,128]{3,2,1,0:T(8,128)(2,1)S(1)} %pad_maximum_fusion.2), channel_id=1, source_target_pairs={{0,6},{2,4},{4,2},{6,0},{8,14},{10,12},{12,10},{14,8},{16,22},{18,... | collective-permute-start | bytes 393224 | tf_op jit(solution)/shard_map/ppermute | solution.py:28

commit v4 on v3

--- a/solution.py
+++ b/solution.py
@@ -156,12 +156,10 @@
     low_row = lax.broadcasted_iota(jnp.int32, (16, wide), 1) < size
     group_range = lax.broadcasted_iota(jnp.int32, (16, groups), 1)
 
-    core = lax.axis_index("aux")
-
     def virt_of(place, slot, part):
         found = virt_ref[place & (turns - 1), place >> bits_of(all_turns), slot & (tiles - 1)]
         turned = jnp.concatenate([found[:, size:], found[:, :size]], axis=1)
-        placed = jnp.where((slot // tiles) ^ core == part, found, turned)
+        placed = jnp.where(slot // tiles == part, found, turned)
         return jnp.where(low if part == 0 else ~low, placed, jnp.zeros_like(placed))
 
     def one(index, total):
@@ -250,7 +248,7 @@
 
     chunks = (5 * pairs // 8,) + (pairs // 8,) * 3 + (pairs // 4,) * 4
     tiles = groups_dev // 2
-    virt = jnp.concatenate([lax.dynamic_slice_in_dim(virtual_blocks, core * tiles, tiles), lax.dynamic_slice_in_dim(virtual_blocks, (1 - core) * tiles, tiles)], axis=2)
+    virt = jnp.concatenate([virtual_blocks[:tiles], virtual_blocks[tiles:]], axis=2)
     other = swap_cores(by_mu(three_centre))
     arrived = [split_flip(virt, near, far, count), split_flip(virt, 0, mid, count)]
     integers = pltpu.SMEM((block_count,), jnp.int32)

time: 31.5 us -> 31.6 us (level)
    dynamic_slice x1 -> x0, local copies, waits for them, and re-layouts: 0.88 us -> none  [body(): lax.dynamic_slice_in_dim(virtual_blocks, core * tiles, tiles)]
    slice x0 -> x1, local copies, waits for them, and re-layouts: none -> 0.88 us  [body(): virtual_blocks[:tiles]]
where the time goes in v4:
time: 31.6 us
  blocking collectives  13.4 us (42%)
  starting transfers between devices  7.3 us (23%)
  Pallas kernels  6.91 us (22%)
  waiting for transfers between devices  2.05 us (6%)
  local copies, waits for them, and re-layouts  1.57 us (5%)
    all_to_all x1, blocking collectives, body(): arrived = lax.all_to_all(partial, ('blk', 'aux'), 0, 0, tiled=True)  13.4 us
    ppermute x3, starting transfers between devices, flip(): lax.ppermute(values, 'blk', [(i, i ^ distance) for i in range(count)])  3.55 us
    ppermute x2, starting transfers between devices, split_flip(): return lax.ppermute(values, ('blk', 'aux'), pairs)  3.29 us
    ppermute x3, waiting for transfers between devices, flip(): lax.ppermute(values, 'blk', [(i, i ^ distance) for i in range(count)])  2.04 us
    pallas_call x1, Pallas kernels, body(): pl.pallas_call(functools.partial(half_kernel, chunks), out_shape=[half_sh...  1.91 us
    pallas_call x1, Pallas kernels, body(): pl.pallas_call(functools.partial(ready_kernel, count, bits_of(all_turns)...  1.69 us
    pallas_call x1, Pallas kernels, body(): pl.pallas_call(functools.partial(early_kernel, chunks), out_shape=jax.Sha...  1.67 us
    pallas_call x1, Pallas kernels, body(): pl.pallas_call(functools.partial(late_kernel, scale, chunks), out_shape=j...  1.64 us
  transfers between devices with their start and end apart: 6, of which 1 were waited for; matrix products, arithmetic and copies ran while one was open for 3% of the time, Pallas kernels for 17%

profile of v4, /device:TPU:0, one launch (start us, length us, event | category | flops | bytes accessed | tf_op | source)
XLA Modules:
  0.0 31.6 jit_solution(1821277086532769961)
XLA Ops:
  0.0 0.5 %collective-permute-start.3 = (bf16[128,64,128]{2,1,0:T(8,128)(2,1)}, bf16[128,64,128]{2,1,0:T(8,128)(2,1)S(1)}, u32[]{:S(2)}, u32[]{:S(2)}) collective-permute-start(bf16[128,64,128]{2,1,0:T(8,128)(2,1)} %bitcast.16), channel_id=1, source_target_pairs={{0,1},{1,0},{2,3},{3,2},{4,5},{5,4},{6,7},{7,6},{8,9},{9,8},{10,11... | collective-permute-start | bytes 6291464 | tf_op jit(solution)/shard_map/ppermute | solution.py:32
  0.5 0.9 %fusion = (bf16[4,64,64]{2,1,0:T(8,128)(2,1)S(1)}, bf16[4,64,64]{2,1,0:T(8,128)(2,1)S(1)}) fusion(bf16[8,64,64]{2,1,0:T(8,128)(2,1)} %param.8), kind=kLoop, calls=%fused_computation.4 | loop fusion | bytes 131072 | tf_op jit(solution)/shard_map/slice | solution.py:251
  1.3 0.0 copy-start
  1.3 0.1 pad_maximum_fusion.3
  1.4 2.6 %collective-permute-start = (bf16[4,64,128]{2,1,0:T(8,128)(2,1)S(1)}, bf16[4,64,128]{2,1,0:T(8,128)(2,1)S(1)}, u32[]{:S(2)}, u32[]{:S(2)}) collective-permute-start(bf16[4,64,128]{2,1,0:T(8,128)(2,1)S(1)} %pad_maximum_fusion.3), channel_id=1, source_target_pairs={{0,8},{1,25},{2,10},{3,27},{4,12},{5,29},{6,14},{7,31},{8,0},{9,17... | collective-permute-start | bytes 196616 | tf_op jit(solution)/shard_map/ppermute | solution.py:37
  4.1 0.7 %collective-permute-start.1 = (bf16[4,64,128]{2,1,0:T(8,128)(2,1)S(1)}, bf16[4,64,128]{2,1,0:T(8,128)(2,1)S(1)}, u32[]{:S(2)}, u32[]{:S(2)}) collective-permute-start(bf16[4,64,128]{2,1,0:T(8,128)(2,1)S(1)} %pad_maximum_fusion.3), channel_id=1, source_target_pairs={{0,0},{1,17},{2,2},{3,19},{4,4},{5,21},{6,6},{7,23},{8,8},{9,25},{... | collective-permute-start | bytes 196616 | tf_op jit(solution)/shard_map/ppermute | solution.py:37
  4.7 1.7 %ready.1 = (bf16[8,128,128]{2,1,0:T(8,128)(2,1)S(1)}, s32[258]{0:T(512)S(4)}, s32[128]{0:T(128)S(4)}, s32[128]{0:T(128)S(4)}, s32[128]{0:T(128)S(4)}) custom-call(s32[128]{0:T(128)} %rows_ref.1, s32[128]{0:T(128)} %slots_ref.1, s32[128]{0:T(128)} %bitcast.25, bf16[8,64,64]{2,1,0:T(8,128)(2,1)} %occ_ref.1), custom_call_target="tpu_custom_call" | custom-call | flops 1000000000 | bytes 4194304 | tf_op jit(solution)/shard_map/ready/pallas_call | solution.py:260
  6.4 0.0 collective-permute-done
  6.5 0.0 collective-permute-done.1
  6.5 1.9 %collective-permute-start.2 = (bf16[2,4,64,128]{3,2,1,0:T(8,128)(2,1)S(1)}, bf16[2,4,64,128]{3,2,1,0:T(8,128)(2,1)S(1)}, u32[]{:S(2)}, u32[]{:S(2)}) collective-permute-start(bf16[2,4,64,128]{3,2,1,0:T(8,128)(2,1)S(1)} %pad_maximum_fusion.2), channel_id=1, source_target_pairs={{0,2},{2,0},{4,6},{6,4},{8,10},{10,8},{12,14},{14,12},{16,18},{18,... | collective-permute-start | bytes 393224 | tf_op jit(solution)/shard_map/ppermute | solution.py:28
  8.4 1.5 %collective-permute-start.4 = (bf16[2,4,64,128]{3,2,1,0:T(8,128)(2,1)S(1)}, bf16[2,4,64,128]{3,2,1,0:T(8,128)(2,1)S(1)}, u32[]{:S(2)}, u32[]{:S(2)}) collective-permute-start(bf16[2,4,64,128]{3,2,1,0:T(8,128)(2,1)S(1)} %pad_maximum_fusion.2), channel_id=1, source_target_pairs={{0,4},{2,6},{4,0},{6,2},{8,12},{10,14},{12,8},{14,10},{16,20},{18,... | collective-permute-start | bytes 393224 | tf_op jit(solution)/shard_map/ppermute | solution.py:28
  9.9 0.2 collective-permute-start.5
  10.0 0.0 collective-permute-done.3.other_ref
  10.0 0.0 copy-done
  10.0 1.9 %half.1 = (bf16[64,128,128]{2,1,0:T(8,128)(2,1)S(1)}, bf16[64,128,128]{2,1,0:T(8,128)(2,1)S(1)}, bf16[64,128,128]{2,1,0:T(8,128)(2,1)S(1)}, bf16[64,128,128]{2,1,0:T(8,128)(2,1)S(1)}) custom-call(s32[258]{0:T(512)S(4)} %get-tuple-element.26.list_ref, s32[128]{0:T(128)S(4)} %get-tuple-element.32.rows, bf16[128,64,128]{2,1,0:T(8,128)(2,1)S(1)} %bitcast.17, ...), custom_call_target="tpu_custom_call" | custom-call | flops 1000000000 | bytes 4194304 | tf_op jit(solution)/shard_map/half/pallas_call | solution.py:278
  12.0 0.0 collective-permute-done.2
  12.0 1.7 %early.1.early_ref = f32[16,64]{1,0:T(8,128)S(1)} custom-call(s32[258]{0:T(512)S(4)} %get-tuple-element.26.list_ref, s32[128]{0:T(128)S(4)} %get-tuple-element.27.slots, s32[128]{0:T(128)S(4)} %get-tuple-element.28.owners, bf16[64,128,128]{2,1,0:T(8,128)(2,1)S(1)} %get-tuple-element.40.own_ref, bf16[64,128,128]{2,1,0:T(8,128)(2,1)S(1)} %get-tuple-element.41.other_ref, ...), custom_call_target="tpu_custom_call" | custom-call | flops 1000000000 | bytes 4194304 | tf_op jit(solution)/shard_map/early/pallas_call | solution.py:294
  13.7 0.0 collective-permute-done.4
  13.7 2.0 %collective-permute-done.5 = bf16[2,4,64,128]{3,2,1,0:T(8,128)(2,1)S(1)} collective-permute-done((bf16[2,4,64,128]{3,2,1,0:T(8,128)(2,1)S(1)}, bf16[2,4,64,128]{3,2,1,0:T(8,128)(2,1)S(1)}, u32[]{:S(2)}, u32[]{:S(2)}) %collective-permute-start.5) | collective-permute-done | bytes 131104 | tf_op jit(solution)/shard_map/ppermute | solution.py:28
  15.8 1.6 %late.1 = f32[32,64]{1,0:T(8,128)S(1)} custom-call(s32[258]{0:T(512)S(4)} %get-tuple-element.26.list_ref, s32[128]{0:T(128)S(4)} %get-tuple-element.27.slots, s32[128]{0:T(128)S(4)} %get-tuple-element.28.owners, bf16[64,128,128]{2,1,0:T(8,128)(2,1)S(1)} %get-tuple-element.38.own_ref, bf16[64,128,128]{2,1,0:T(8,128)(2,1)S(1)} %get-tuple-element.39.other_ref, ...), custom_call_target="tpu_custom_call" | custom-call | flops 1000000000 | bytes 4194304 | tf_op jit(solution)/shard_map/late/pallas_call | solution.py:303
  17.4 13.4 %all_to_all.9 = f32[32,1,64]{2,1,0:T(1,128)S(1)} all-to-all(f32[32,1,64]{2,1,0:T(1,128)S(1)} %bitcast.18), channel_id=1, replica_groups=mesh['blk'=16,'aux'=2] {'blk','aux'}, dimensions={0} | all-to-all | bytes 16384 | tf_op jit(solution)/shard_map/all_to_all | solution.py:313
  30.8 0.1 reduce_sum.9
  30.9 0.7 %reshape.19 = f32[2,4,8]{2,1,0:T(4,128)} reshape(f32[64]{0:T(128)S(1)} %reduce_sum.9) | data formatting | bytes 512 | tf_op jit(solution)/shard_map/reshape | solution.py:314
  (3 shorter events, 0.1 us)
Async XLA Ops:
  0.0 10.0 %collective-permute-start.3 = (bf16[128,64,128]{2,1,0:T(8,128)(2,1)}, bf16[128,64,128]{2,1,0:T(8,128)(2,1)S(1)}, u32[]{:S(2)}, u32[]{:S(2)}) collective-permute-start(bf16[128,64,128]{2,1,0:T(8,128)(2,1)} %bitcast.16), channel_id=1, source_target_pairs={{0,1},{1,0},{2,3},{3,2},{4,5},{5,4},{6,7},{7,6},{8,9},{9,8},{10,11... | collective-permute-start | bytes 6291464 | tf_op jit(solution)/shard_map/ppermute | solution.py:32
  1.3 8.7 %copy-start = (bf16[128,2,4096]{2,1,0:T(2,128)(2,1)S(1)}, bf16[128,2,4096]{2,1,0:T(2,128)(2,1)}, u32[]{:S(2)}) copy-start(bf16[128,2,4096]{2,1,0:T(2,128)(2,1)} %param.6) | copy-start | bytes 6291460
  1.4 5.0 %collective-permute-start = (bf16[4,64,128]{2,1,0:T(8,128)(2,1)S(1)}, bf16[4,64,128]{2,1,0:T(8,128)(2,1)S(1)}, u32[]{:S(2)}, u32[]{:S(2)}) collective-permute-start(bf16[4,64,128]{2,1,0:T(8,128)(2,1)S(1)} %pad_maximum_fusion.3), channel_id=1, source_target_pairs={{0,8},{1,25},{2,10},{3,27},{4,12},{5,29},{6,14},{7,31},{8,0},{9,17... | collective-permute-start | bytes 196616 | tf_op jit(solution)/shard_map/ppermute | solution.py:37
  4.1 2.4 %collective-permute-start.1 = (bf16[4,64,128]{2,1,0:T(8,128)(2,1)S(1)}, bf16[4,64,128]{2,1,0:T(8,128)(2,1)S(1)}, u32[]{:S(2)}, u32[]{:S(2)}) collective-permute-start(bf16[4,64,128]{2,1,0:T(8,128)(2,1)S(1)} %pad_maximum_fusion.3), channel_id=1, source_target_pairs={{0,0},{1,17},{2,2},{3,19},{4,4},{5,21},{6,6},{7,23},{8,8},{9,25},{... | collective-permute-start | bytes 196616 | tf_op jit(solution)/shard_map/ppermute | solution.py:37
  6.5 5.5 %collective-permute-start.2 = (bf16[2,4,64,128]{3,2,1,0:T(8,128)(2,1)S(1)}, bf16[2,4,64,128]{3,2,1,0:T(8,128)(2,1)S(1)}, u32[]{:S(2)}, u32[]{:S(2)}) collective-permute-start(bf16[2,4,64,128]{3,2,1,0:T(8,128)(2,1)S(1)} %pad_maximum_fusion.2), channel_id=1, source_target_pairs={{0,2},{2,0},{4,6},{6,4},{8,10},{10,8},{12,14},{14,12},{16,18},{18,... | collective-permute-start | bytes 393224 | tf_op jit(solution)/shard_map/ppermute | solution.py:28
  8.4 5.3 %collective-permute-start.4 = (bf16[2,4,64,128]{3,2,1,0:T(8,128)(2,1)S(1)}, bf16[2,4,64,128]{3,2,1,0:T(8,128)(2,1)S(1)}, u32[]{:S(2)}, u32[]{:S(2)}) collective-permute-start(bf16[2,4,64,128]{3,2,1,0:T(8,128)(2,1)S(1)} %pad_maximum_fusion.2), channel_id=1, source_target_pairs={{0,4},{2,6},{4,0},{6,2},{8,12},{10,14},{12,8},{14,10},{16,20},{18,... | collective-permute-start | bytes 393224 | tf_op jit(solution)/shard_map/ppermute | solution.py:28
  9.9 5.9 %collective-permute-start.5 = (bf16[2,4,64,128]{3,2,1,0:T(8,128)(2,1)S(1)}, bf16[2,4,64,128]{3,2,1,0:T(8,128)(2,1)S(1)}, u32[]{:S(2)}, u32[]{:S(2)}) collective-permute-start(bf16[2,4,64,128]{3,2,1,0:T(8,128)(2,1)S(1)} %pad_maximum_fusion.2), channel_id=1, source_target_pairs={{0,6},{2,4},{4,2},{6,0},{8,14},{10,12},{12,10},{14,8},{16,22},{18,... | collective-permute-start | bytes 393224 | tf_op jit(solution)/shard_map/ppermute | solution.py:28
